TPU v7x, 32 devices: a whole 2x2x4 slice. The times are simulated.
32 devices in a mesh: dp: 8 (over z, y), seq: 4 (over x, core).
Axes of the slice: x: 2, y: 2, z: 4, core: 2. Of those that a mesh axis runs over, the one named last changes fastest.
Arguments:
- frames: bfloat16 [16, 512, 1024], P('dp', 'seq'), may hold values from -6 to 6
- lengths: int32 [16], P('dp'), may hold values from 128 to 512, as said below
- qkv_weight: bfloat16 [1024, 3072], P('dp'), may hold values from -8 to 8, as said below
- out_weight: bfloat16 [1024, 1024], P('dp'), may hold values from -0.75 to 0.75
- cotangent: bfloat16 [16, 512, 1024], P('dp', 'seq'), may hold values from -6 to 6
Outputs:
- result: bfloat16 [16, 512, 1024], P('dp', 'seq')
- frame_grad: bfloat16 [16, 512, 1024], P('dp', 'seq')
- qkv_weight_grad: float32 [1024, 3072], P('dp')
- out_weight_grad: float32 [1024, 1024], P('dp')
Inputs may be any that keep to these rules, and one draw needn't show every extreme that they name: `lengths`: valid frames of each recording; in every draw some recording is valid over the whole slab. `qkv_weight`: a projection.
All inputs are finite; a program needn't handle non-finite values.
Results may differ from a plain program's by a relative error of at most 0.023.
The roundings to bfloat16 on the way count: a program that leaves them out, or rounds other values in their place, can miss the bound.
Values may be sent and summed in bfloat16 or wider, within the bound.
A program may use at most 128 MiB of HBM per device.

v0:
```python
import math

import jax
import jax.numpy as jnp
from jax import lax
from jax.sharding import PartitionSpec as P

H = 16
GROUP = 16
LEFT = 64
AHEAD = 4


def from_behind(value, axis, steps):
    count = lax.axis_size(axis)
    initial, last = (max(0, -steps), min(count, count - steps))
    return lax.ppermute(value, axis, [(source, source + steps) for source in range(initial, last)])


def norm_rows(frames):
    as_float = frames.astype(jnp.float32)
    row_mean = jnp.mean(as_float, axis=-1, keepdims=True)
    centred = as_float - row_mean
    variance = jnp.mean(centred * centred, axis=-1, keepdims=True)
    inv_std = lax.rsqrt(variance + 1e-05)
    return (centred * inv_std, inv_std)


def window_mask(query_pos, key_pos, lengths, slab_len):
    group_start = query_pos // GROUP * GROUP
    inside = (key_pos[None, :] >= 0) & (key_pos[None, :] < slab_len)
    inside = inside & (key_pos[None, :] >= group_start[:, None] - LEFT)
    inside = inside & (key_pos[None, :] < group_start[:, None] + GROUP + AHEAD)
    allowed = (key_pos[None, None, :] < lengths[:, None, None]) | (
        query_pos[None, :, None] >= lengths[:, None, None]
    )
    return inside[None] & allowed


def attend(queries, key_rows, value_rows, allowed_mask, score_scale):
    scores = (
        jnp.einsum("bfhe,bkhe->bhfk", queries, key_rows, preferred_element_type=jnp.float32)
        * score_scale
    )
    wide_mask = allowed_mask[:, None]
    scores = jnp.where(wide_mask, scores, -1e30)
    row_max = jnp.max(scores, axis=-1, keepdims=True)
    shifted = jnp.where(wide_mask, jnp.exp(scores - row_max), 0.0)
    attn_probs = shifted / jnp.sum(shifted, axis=-1, keepdims=True)
    probs_half = attn_probs.astype(jnp.bfloat16)
    mixed_rows = jnp.einsum(
        "bhfk,bkhe->bfhe", probs_half, value_rows, preferred_element_type=jnp.float32
    )
    return (mixed_rows.astype(jnp.bfloat16), attn_probs, probs_half)


def attend_back(queries, key_rows, value_rows, attn_probs, probs_half, mixed_grad, score_scale):
    value_grad = jnp.einsum(
        "bhfk,bfhe->bkhe", probs_half, mixed_grad, preferred_element_type=jnp.float32
    )
    prob_grad = jnp.einsum(
        "bfhe,bkhe->bhfk", mixed_grad, value_rows, preferred_element_type=jnp.float32
    )
    score_grad = (
        attn_probs
        * (prob_grad - jnp.sum(attn_probs * prob_grad, axis=-1, keepdims=True))
        * score_scale
    )
    score_grad = score_grad.astype(jnp.bfloat16)
    query_grad = jnp.einsum(
        "bhfk,bkhe->bfhe", score_grad, key_rows, preferred_element_type=jnp.float32
    )
    key_grad = jnp.einsum(
        "bhfk,bfhe->bkhe", score_grad, queries, preferred_element_type=jnp.float32
    )
    return (query_grad, key_grad, value_grad)


def per_device(frames, lengths, qkv_weight, out_weight, cotangent):
    records, frame_count, model_width = frames.shape
    head_count = H
    head_size = model_width // head_count
    row_count = records * frame_count
    seq_size = lax.axis_size("seq")
    slab_len = frame_count * seq_size
    frame_base = lax.axis_index("seq") * frame_count
    score_scale = 1.0 / math.sqrt(head_size)
    span_len = frame_count + LEFT + AHEAD
    qkv_full = lax.all_gather(qkv_weight, "dp", axis=0, tiled=True)
    centred, inv_std = norm_rows(frames)
    normed = centred.astype(jnp.bfloat16)
    normed_flat = normed.reshape(row_count, model_width)
    projected_qkv = jnp.dot(normed_flat, qkv_full, preferred_element_type=jnp.float32)
    projected_qkv = projected_qkv.astype(jnp.bfloat16).reshape(
        records, frame_count, 3 * model_width
    )
    key_value = projected_qkv[:, :, model_width:]
    left_rows = from_behind(key_value[:, frame_count - LEFT :], "seq", 1)
    right_rows = from_behind(key_value[:, :AHEAD], "seq", -1)
    extended = jnp.concatenate([left_rows, key_value, right_rows], axis=1)
    queries = projected_qkv[:, :, :model_width].reshape(records, frame_count, head_count, head_size)
    key_rows = extended[:, :, :model_width].reshape(records, span_len, head_count, head_size)
    value_rows = extended[:, :, model_width:].reshape(records, span_len, head_count, head_size)
    query_pos = frame_base + jnp.arange(frame_count, dtype=jnp.int32)
    key_pos = frame_base - LEFT + jnp.arange(span_len, dtype=jnp.int32)
    allowed_mask = window_mask(query_pos, key_pos, lengths, slab_len)
    mixed_rows, attn_probs, probs_half = attend(
        queries, key_rows, value_rows, allowed_mask, score_scale
    )
    mixed_flat = mixed_rows.reshape(row_count, model_width)
    out_full = lax.all_gather(out_weight, "dp", axis=0, tiled=True)
    projected = jnp.dot(mixed_flat, out_full, preferred_element_type=jnp.float32).reshape(
        records, frame_count, model_width
    )
    is_valid = (query_pos[None, :] < lengths[:, None])[:, :, None]
    result = jnp.where(is_valid, projected, 0.0).astype(jnp.bfloat16)
    out_grad = jnp.where(is_valid, cotangent, jnp.zeros_like(cotangent))
    out_grad_flat = out_grad.reshape(row_count, model_width)
    mixed_grad = lax.dot_general(
        out_grad_flat, out_full, (((1,), (1,)), ((), ())), preferred_element_type=jnp.float32
    )
    mixed_grad = mixed_grad.astype(jnp.bfloat16).reshape(
        records, frame_count, head_count, head_size
    )
    query_grad, key_grad, value_grad = attend_back(
        queries, key_rows, value_rows, attn_probs, probs_half, mixed_grad, score_scale
    )
    pair_grad = jnp.concatenate(
        [
            key_grad.reshape(records, span_len, model_width),
            value_grad.reshape(records, span_len, model_width),
        ],
        axis=-1,
    )
    from_right = from_behind(pair_grad[:, :LEFT], "seq", -1)
    from_left = from_behind(pair_grad[:, LEFT + frame_count :], "seq", 1)
    own_grad = pair_grad[:, LEFT : LEFT + frame_count]
    own_grad = own_grad.at[:, frame_count - LEFT :].add(from_right)
    own_grad = own_grad.at[:, :AHEAD].add(from_left)
    query_half = query_grad.reshape(records, frame_count, model_width).astype(jnp.bfloat16)
    qkv_grad = jnp.concatenate([query_half, own_grad.astype(jnp.bfloat16)], axis=-1).reshape(
        row_count, 3 * model_width
    )
    columns = normed_flat
    part_qkv = lax.psum_scatter(
        lax.dot_general(
            columns, qkv_grad, (((0,), (0,)), ((), ())), preferred_element_type=jnp.float32
        ),
        "dp",
        scatter_dimension=0,
        tiled=True,
    )
    columns = mixed_flat
    part_out = lax.psum_scatter(
        lax.dot_general(
            columns, out_grad_flat, (((0,), (0,)), ((), ())), preferred_element_type=jnp.float32
        ),
        "dp",
        scatter_dimension=0,
        tiled=True,
    )
    qkv_weight_grad, out_weight_grad = lax.psum((part_qkv, part_out), "seq")
    norm_grad = lax.dot_general(
        qkv_grad, qkv_full, (((1,), (1,)), ((), ())), preferred_element_type=jnp.float32
    )
    norm_grad = norm_grad.reshape(records, frame_count, model_width)
    mean_one = jnp.mean(norm_grad, axis=-1, keepdims=True)
    mean_two = jnp.mean(norm_grad * centred, axis=-1, keepdims=True)
    frame_grad = ((norm_grad - mean_one - centred * mean_two) * inv_std).astype(jnp.bfloat16)
    return (result, frame_grad, qkv_weight_grad, out_weight_grad)


def solution(mesh):
    in_specs = (P("dp", "seq", None), P("dp"), P("dp", None), P("dp", None), P("dp", "seq", None))
    out_specs = (P("dp", "seq", None), P("dp", "seq", None), P("dp", None), P("dp", None))
    return jax.shard_map(
        per_device, mesh=mesh, in_specs=in_specs, out_specs=out_specs, check_vma=False
    )
```

profile of v0, /device:TPU:0, one launch (start us, length us, event | category | flops | bytes accessed | tf_op | source)
XLA Modules:
  0.0 526.0 jit_solution(15544554087649004221)
XLA Ops:
  8.7 1.2 convert_reduce_fusion
  9.9 1.3 fusion.40
  12.2 1.3 fusion.35
  13.4 98.5 %all-gather.3.cloned.1.call-done = bf16[1024,3072]{1,0:T(8,128)(2,1)} async-done(((bf16[128,3072]{1,0:T(8,128)(2,1)}), bf16[1024,3072]{1,0:T(8,128)(2,1)}) %all-gather.3.cloned.1.call-update) | async-done | bytes 6291472 | tf_op jit(solution)/shard_map/all_gather | solution.py:89
  111.9 4.6 convolution_convert_fusion
  116.6 1.3 collective-permute-start
  118.2 1.3 collective-permute-start.1
  120.8 2.2 collective-permute-done.1
  123.2 1.3 copy.21
  125.0 4.8 fusion.65
  129.8 2.7 convolution_convert_fusion.1
  133.9 2.7 fusion.48
  136.8 24.7 %all-gather.5.cloned.1.call-done = bf16[1024,1024]{1,0:T(8,128)(2,1)} async-done(((bf16[128,1024]{1,0:T(8,128)(2,1)}), bf16[1024,1024]{1,0:T(8,128)(2,1)}) %all-gather.5.cloned.1.call-update) | async-done | bytes 2097168 | tf_op jit(solution)/shard_map/all_gather | solution.py:111
  161.6 2.3 convolution_convert_fusion.2
  165.4 4.4 fusion.45
  169.9 2.2 copy.27
  172.1 2.8 fusion.66
  174.9 7.5 %fusion.12 = f32[2,16,64,196]{3,2,1,0:T(8,128)} fusion(bf16[2,128,16,64]{1,3,2,0:T(8,128)(2,1)} %bitcast.73, f32[2,16,128,196]{2,3,1,0:T(8,128)} %fusion.66, f32[2,16,128,196]{2,3,1,0:T(8,128)} %get-tuple-element.37, f32[2,16,128]{2,1,0:T(8,128)S(1)} %get-tuple-element.36), kind=kOutput, calls=%fused_computation.21 | convolution fusion | flops 108384448 | bytes 8568832 | tf_op jit(solution)/shard_map/bhfk,bfhe->bkhe/dot_general | solution.py:73
  182.4 1.9 copy.26
  185.4 1.3 collective-permute-start.2
  186.7 7.5 %fusion.25 = bf16[2,16,64,128]{3,2,1,0:T(8,128)(2,1)} fusion(bf16[2,196,16,64]{1,3,2,0:T(8,128)(2,1)} %bitcast.71, f32[2,16,128,196]{2,3,1,0:T(8,128)} %fusion.66, f32[2,16,128,196]{2,3,1,0:T(8,128)} %get-tuple-element.37, f32[2,16,128]{2,1,0:T(8,128)S(1)} %get-tuple-element.36), kind=kOutput, calls=%fused_computation.34 | convolution fusion | flops 108646592 | bytes 7766016 | tf_op jit(solution)/shard_map/bhfk,bkhe->bfhe/dot_general | solution.py:70
  194.2 2.0 copy.28
  196.3 3.0 collective-permute-start.3
  199.4 1.4 fusion.44
  201.1 6.4 %convolution_bitcast_fusion = f32[1024,3072]{1,0:T(8,128)} fusion(bf16[2,128,1024]{2,1,0:T(8,128)(2,1)S(1)} %copy-done.2, bf16[2,128,2048]{2,1,0:T(8,128)(2,1)S(1)} %convert_element_type.54, bf16[2,128,1024]{2,1,0:T(8,128)(2,1)S(1)} %copy-done.3), kind=kOutput, calls=%fused_computation.2 | convolution fusion | flops 1613758464 | bytes 14680064 | tf_op jit(solution)/shard_map/dot_general | solution.py:146
  208.6 3.1 fusion.28
  211.7 40.1 %reduce-scatter.5.cloned.1.call-done = f32[128,1024]{1,0:T(8,128)} async-done(((f32[1024,1024]{1,0:T(8,128)}), f32[128,1024]{1,0:T(8,128)}) %reduce-scatter.5.cloned.1.call-update) | async-done | bytes 524304 | tf_op jit(solution)/shard_map/reduce_scatter | solution.py:154
  251.8 211.0 %reduce-scatter.3.cloned.1.call-done = f32[128,3072]{1,0:T(8,128)} async-done(((f32[1024,3072]{1,0:T(8,128)}), f32[128,3072]{1,0:T(8,128)}) %reduce-scatter.3.cloned.1.call-update) | async-done | bytes 1572880 | tf_op jit(solution)/shard_map/reduce_scatter | solution.py:145
  462.9 4.8 fusion.63
  467.6 1.2 fusion.39
  468.8 47.1 %all-reduce.3.cloned.1.call-done = (f32[128,3072]{1,0:T(8,128)}, f32[128,1024]{1,0:T(8,128)}) async-done(((f32[128,3072]{1,0:T(8,128)}, f32[128,1024]{1,0:T(8,128)}), (f32[128,3072]{1,0:T(8,128)}, f32[128,1024]{1,0:T(8,128)})) %all-reduce.3.cloned.1.call-update) | async-done | bytes 2097168 | tf_op jit(solution)/shard_map/psum | solution.py:162
  515.9 2.8 copy.44
  (63 shorter events, 11.0 us)
Async XLA Ops:
  7.2 104.8 %all-gather.3.cloned.1.call-start = ((), (), s32[]{:S(2)}) async-start(), calls=%async_computation.2 | async-start | bytes 7077888 | tf_op jit(solution)/shard_map/all_gather | solution.py:89
  7.9 153.7 %all-gather.5.cloned.1.call-start = ((), (), s32[]{:S(2)}) async-start(), calls=%async_computation.3 | async-start | bytes 2359296 | tf_op jit(solution)/shard_map/all_gather | solution.py:111
  8.6 243.1 %reduce-scatter.5.cloned.1.call-start = ((), (), s32[]{:S(2)}) async-start(), calls=%async_computation.5 | async-start | bytes 4718592 | tf_op jit(solution)/shard_map/reduce_scatter | solution.py:154
  13.4 103.2 %copy-start.1 = (bf16[2,128,1024]{2,1,0:T(8,128)(2,1)}, bf16[2,128,1024]{2,1,0:T(8,128)(2,1)S(1)}, u32[]{:S(2)}) copy-start(bf16[2,128,1024]{2,1,0:T(8,128)(2,1)S(1)} %fusion.35) | copy-start | bytes 1572868
  111.9 6.0 %copy-start.9 = (s32[2]{0:T(128)S(1)}, s32[2]{0:T(128)}, u32[]{:S(2)}) copy-start(s32[2]{0:T(128)} %param.10) | copy-start | bytes 28
  111.9 6.1 %copy-start.8 = (bf16[2,128,1024]{2,1,0:T(8,128)(2,1)S(1)}, bf16[2,128,1024]{2,1,0:T(8,128)(2,1)}, u32[]{:S(2)}) copy-start(bf16[2,128,1024]{2,1,0:T(8,128)(2,1)} %param.13) | copy-start | bytes 1572868
  116.6 6.3 %collective-permute-start = (bf16[2,64,2048]{2,1,0:T(8,128)(2,1)S(1)}, bf16[2,64,2048]{2,1,0:T(8,128)(2,1)S(1)}, u32[]{:S(2)}, u32[]{:S(2)}) collective-permute-start(bf16[2,64,2048]{2,1,0:T(8,128)(2,1)S(1)} %slice.89), channel_id=1, source_target_pairs={{0,1},{1,2},{2,3},{4,5},{5,6},{6,7},{8,9},{9,10},{10,11},{12,13},{... | collective-permute-start | bytes 1572872 | tf_op jit(solution)/shard_map/ppermute | solution.py:17
  118.2 4.8 collective-permute-start.1
  132.5 0.8 copy-start.5
  136.6 326.2 %reduce-scatter.3.cloned.1.call-start = ((), (), s32[]{:S(2)}) async-start(), calls=%async_computation.4 | async-start | bytes 14155776 | tf_op jit(solution)/shard_map/reduce_scatter | solution.py:145
  185.4 14.0 %collective-permute-start.2 = (f32[2,64,2048]{2,1,0:T(8,128)}, f32[2,64,2048]{2,1,0:T(8,128)}, u32[]{:S(2)}, u32[]{:S(2)}) collective-permute-start(f32[2,64,2048]{2,1,0:T(8,128)} %fusion.41), channel_id=1, source_target_pairs={{1,0},{2,1},{3,2},{5,4},{6,5},{7,6},{9,8},{10,9},{11,10},{13,12},{... | collective-permute-start | bytes 3145736 | tf_op jit(solution)/shard_map/ppermute | solution.py:17
  196.3 4.6 collective-permute-start.3
  199.4 1.7 copy-start.2
  199.4 1.7 copy-start.3
  207.5 1.1 copy-start.6
  207.5 255.3 %copy-start = (bf16[2,128,1024]{2,1,0:T(8,128)(2,1)S(1)}, bf16[2,128,1024]{2,1,0:T(8,128)(2,1)}, u32[]{:S(2)}) copy-start(bf16[2,128,1024]{2,1,0:T(8,128)(2,1)} %param.9) | copy-start | bytes 1572868
  207.5 255.3 %copy-start.4 = (bf16[2,128,1024]{2,1,0:T(8,128)(2,1)S(1)}, bf16[2,128,1024]{2,1,0:T(8,128)(2,1)}, u32[]{:S(2)}) copy-start(bf16[2,128,1024]{2,1,0:T(8,128)(2,1)} %copy.28) | copy-start | bytes 1572868
  207.6 308.3 %all-reduce.3.cloned.1.call-start = ((), (), s32[]{:S(2)}) async-start(), calls=%async_computation.6 | async-start | bytes 4194304 | tf_op jit(solution)/shard_map/psum | solution.py:162
  515.9 2.8 copy-start.7
Sparse Core Ops, SparseCore 0:
  10.2 101.7 all-gather.2
  114.1 47.4 all-gather.4
  165.2 86.5 reduce-scatter.4
  255.7 207.1 reduce-scatter.2
  465.2 50.6 all-reduce.2
where the time goes:
time: 527 us; the launch traced here: 526 us
  waiting for transfers between devices  425 us (81%)
  matrix products  53.7 us (10%)
  local copies, waits for them, and re-layouts  16.7 us (3%)
  between operations  14.1 us (3%)
  other arithmetic  9.1 us (2%)
  starting transfers between devices  7.27 us (1%)
    reduce_scatter x1, waiting for transfers between devices, per_device(): lax.psum_scatter(lax.dot_general(columns, qkv_grad, (((0,), (0,)), ((), (...  211 us
    all_gather x1, waiting for transfers between devices, per_device(): qkv_full = lax.all_gather(qkv_weight, 'dp', axis=0, tiled=True)  98.5 us
    psum x1, waiting for transfers between devices, per_device(): qkv_weight_grad, out_weight_grad = lax.psum((part_qkv, part_out), 'seq')  47.1 us
    reduce_scatter x1, waiting for transfers between devices, per_device(): lax.psum_scatter(lax.dot_general(columns, out_grad_flat, (((0,), (0,)), (...  40.1 us
    all_gather x1, waiting for transfers between devices, per_device(): out_full = lax.all_gather(out_weight, 'dp', axis=0, tiled=True)  24.7 us
  transfers between devices with their start and end apart: 9, of which 6 were waited for; matrix products, arithmetic and copies ran while one was open for 14% of the time, Pallas kernels for 0%

commit v1 on v0

v1 whole, which is shorter than its diff:
```python
import math

import jax
import jax.numpy as jnp
from jax import lax
from jax.sharding import PartitionSpec as P

H = 16
GROUP = 16
LEFT = 64
AHEAD = 4
BLOCK = 128


def norm_rows(frames):
    as_float = frames.astype(jnp.float32)
    row_mean = jnp.mean(as_float, axis=-1, keepdims=True)
    centred = as_float - row_mean
    variance = jnp.mean(centred * centred, axis=-1, keepdims=True)
    inv_std = lax.rsqrt(variance + 1e-05)
    return (centred * inv_std, inv_std)


def window_mask(query_pos, key_pos, lengths, slab_len):
    group_start = query_pos // GROUP * GROUP
    inside = (key_pos[None, :] >= 0) & (key_pos[None, :] < slab_len)
    inside = inside & (key_pos[None, :] >= group_start[:, None] - LEFT)
    inside = inside & (key_pos[None, :] < group_start[:, None] + GROUP + AHEAD)
    allowed = (key_pos[None, None, :] < lengths[:, None, None]) | (
        query_pos[None, :, None] >= lengths[:, None, None]
    )
    return inside[None] & allowed


def attend(queries, key_rows, value_rows, allowed_mask, score_scale):
    scores = (
        jnp.einsum("bfhe,bkhe->bhfk", queries, key_rows, preferred_element_type=jnp.float32)
        * score_scale
    )
    wide_mask = allowed_mask[:, None]
    scores = jnp.where(wide_mask, scores, -1e30)
    row_max = jnp.max(scores, axis=-1, keepdims=True)
    shifted = jnp.where(wide_mask, jnp.exp(scores - row_max), 0.0)
    attn_probs = shifted / jnp.sum(shifted, axis=-1, keepdims=True)
    probs_half = attn_probs.astype(jnp.bfloat16)
    mixed_rows = jnp.einsum(
        "bhfk,bkhe->bfhe", probs_half, value_rows, preferred_element_type=jnp.float32
    )
    return (mixed_rows.astype(jnp.bfloat16), attn_probs, probs_half)


def attend_back(queries, key_rows, value_rows, attn_probs, probs_half, mixed_grad, score_scale):
    value_grad = jnp.einsum(
        "bhfk,bfhe->bkhe", probs_half, mixed_grad, preferred_element_type=jnp.float32
    )
    prob_grad = jnp.einsum(
        "bfhe,bkhe->bhfk", mixed_grad, value_rows, preferred_element_type=jnp.float32
    )
    score_grad = (
        attn_probs
        * (prob_grad - jnp.sum(attn_probs * prob_grad, axis=-1, keepdims=True))
        * score_scale
    )
    score_grad = score_grad.astype(jnp.bfloat16)
    query_grad = jnp.einsum(
        "bhfk,bkhe->bfhe", score_grad, key_rows, preferred_element_type=jnp.float32
    )
    key_grad = jnp.einsum(
        "bhfk,bfhe->bkhe", score_grad, queries, preferred_element_type=jnp.float32
    )
    return (query_grad, key_grad, value_grad)


def per_device(frames, lengths, qkv_weight, out_weight, cotangent):
    records, frame_count, model_width = frames.shape
    head_size = model_width // H
    seq_size = lax.axis_size("seq")
    seq_index = lax.axis_index("seq")
    wide = model_width // seq_size
    heads = wide // head_size
    slab_len = frame_count * seq_size
    row_count = records * slab_len
    blocks = slab_len // BLOCK
    span = BLOCK + LEFT + AHEAD
    score_scale = 1.0 / math.sqrt(head_size)

    shard_rows = qkv_weight.shape[0]
    qkv_mine = lax.dynamic_index_in_dim(
        qkv_weight.reshape(shard_rows, 3, seq_size, wide), seq_index, 2, False
    ).reshape(shard_rows, 3 * wide)
    out_mine = lax.dynamic_slice_in_dim(out_weight, seq_index * wide, wide, 1)
    weights = lax.all_gather(
        jnp.concatenate([qkv_mine, out_mine], axis=1), "dp", axis=0, tiled=True
    )
    both = lax.all_gather(
        jnp.stack([frames, cotangent]), "seq", axis=2, tiled=True
    )
    qkv_cols = weights[:, : 3 * wide]
    out_rows = lax.all_to_all(
        weights[:, 3 * wide :].reshape(seq_size, wide, wide), "seq", 0, 0
    )
    out_rows = jnp.swapaxes(out_rows, 0, 1).reshape(wide, model_width)

    centred, _ = norm_rows(both[0])
    normed = centred.astype(jnp.bfloat16).reshape(row_count, model_width)
    positions = jnp.arange(slab_len, dtype=jnp.int32)
    is_valid = (positions[None, :] < lengths[:, None])[:, :, None]
    out_grad = jnp.where(is_valid, both[1], jnp.zeros_like(both[1])).reshape(row_count, model_width)

    qkv = jnp.dot(normed, qkv_cols, preferred_element_type=jnp.float32).astype(jnp.bfloat16)
    qkv = qkv.reshape(records, slab_len, 3, heads, head_size)
    queries = qkv[:, :, 0].reshape(records * blocks, BLOCK, heads, head_size)

    def windows(value):
        padded = jnp.pad(value, ((0, 0), (LEFT, AHEAD), (0, 0), (0, 0)))
        cut = [padded[:, b * BLOCK : b * BLOCK + span] for b in range(blocks)]
        return jnp.stack(cut, axis=1).reshape(records * blocks, span, heads, head_size)

    key_rows, value_rows = windows(qkv[:, :, 1]), windows(qkv[:, :, 2])
    masks = []
    for b in range(blocks):
        query_pos = b * BLOCK + jnp.arange(BLOCK, dtype=jnp.int32)
        key_pos = b * BLOCK - LEFT + jnp.arange(span, dtype=jnp.int32)
        masks.append(window_mask(query_pos, key_pos, lengths, slab_len))
    allowed_mask = jnp.stack(masks, axis=1).reshape(records * blocks, BLOCK, span)
    mixed, attn_probs, probs_half = attend(
        queries, key_rows, value_rows, allowed_mask, score_scale
    )
    mixed_flat = mixed.reshape(row_count, wide)
    partial = jnp.dot(mixed_flat, out_rows, preferred_element_type=jnp.float32)
    partial = partial.astype(jnp.bfloat16).reshape(records, slab_len, model_width)
    result = lax.psum_scatter(partial, "seq", scatter_dimension=1, tiled=True)
    own_pos = seq_index * frame_count + jnp.arange(frame_count, dtype=jnp.int32)
    own_valid = (own_pos[None, :] < lengths[:, None])[:, :, None]
    result = jnp.where(own_valid, result, jnp.zeros_like(result))

    mixed_grad = lax.dot_general(
        out_grad, out_rows, (((1,), (1,)), ((), ())), preferred_element_type=jnp.float32
    )
    mixed_grad = mixed_grad.astype(jnp.bfloat16).reshape(records * blocks, BLOCK, heads, head_size)
    query_grad, key_grad, value_grad = attend_back(
        queries, key_rows, value_rows, attn_probs, probs_half, mixed_grad, score_scale
    )

    def fold(value):
        value = value.reshape(records, blocks, span, wide)
        total = value[:, :, LEFT : LEFT + BLOCK]
        total = total.at[:, :-1, BLOCK - LEFT :].add(value[:, 1:, :LEFT])
        total = total.at[:, 1:, :AHEAD].add(value[:, :-1, LEFT + BLOCK :])
        return total.reshape(row_count, wide).astype(jnp.bfloat16)

    qkv_grad = jnp.concatenate(
        [query_grad.reshape(row_count, wide).astype(jnp.bfloat16), fold(key_grad), fold(value_grad)],
        axis=1,
    )
    norm_part = lax.dot_general(
        qkv_grad, qkv_cols, (((1,), (1,)), ((), ())), preferred_element_type=jnp.float32
    )
    norm_part = norm_part.astype(jnp.bfloat16).reshape(records, slab_len, model_width)
    norm_grad = lax.psum_scatter(norm_part, "seq", scatter_dimension=1, tiled=True)
    norm_grad = norm_grad.astype(jnp.float32)
    part_out = lax.dot_general(
        mixed_flat, out_grad, (((0,), (0,)), ((), ())), preferred_element_type=jnp.float32
    ).astype(jnp.bfloat16)
    part_out = lax.all_to_all(
        jnp.swapaxes(part_out.reshape(wide, seq_size, wide), 0, 1), "seq", 0, 0
    ).reshape(model_width, wide)
    part_qkv = lax.dot_general(
        normed, qkv_grad, (((0,), (0,)), ((), ())), preferred_element_type=jnp.float32
    ).astype(jnp.bfloat16)
    part = jnp.concatenate([part_qkv, part_out], axis=1)
    part = lax.psum_scatter(part, "dp", scatter_dimension=0, tiled=True)
    full = lax.all_gather(part, "seq", axis=0)
    full = full.reshape(seq_size, shard_rows, 4, wide).astype(jnp.float32)
    full = full.transpose(1, 2, 0, 3).reshape(shard_rows, 4 * model_width)
    qkv_weight_grad = full[:, : 3 * model_width]
    out_weight_grad = full[:, 3 * model_width :]

    centred, inv_std = norm_rows(frames)
    mean_one = jnp.mean(norm_grad, axis=-1, keepdims=True)
    mean_two = jnp.mean(norm_grad * centred, axis=-1, keepdims=True)
    frame_grad = ((norm_grad - mean_one - centred * mean_two) * inv_std).astype(jnp.bfloat16)
    return (result, frame_grad, qkv_weight_grad, out_weight_grad)


def solution(mesh):
    in_specs = (P("dp", "seq", None), P("dp"), P("dp", None), P("dp", None), P("dp", "seq", None))
    out_specs = (P("dp", "seq", None), P("dp", "seq", None), P("dp", None), P("dp", None))
    return jax.shard_map(
        per_device, mesh=mesh, in_specs=in_specs, out_specs=out_specs, check_vma=False
    )
```

time: 527 us -> 378 us (0.72)
  waiting for transfers between devices: 425 us -> 222 us
  local copies, waits for them, and re-layouts: 16.7 us -> 62.1 us
  other arithmetic: 9.1 us -> 31.8 us
  matrix products: 53.7 us -> 38.7 us
    reduce_scatter x2, waiting for transfers between devices: 251 us -> 63.2 us  [the longest x1 32.5 us: per_device(): result = lax.psum_scatter(partial, 'seq', scatter_dimension=1, tiled=True)]
    unnamed x5 -> x7, waiting for transfers between devices: 1.43 us -> 57.7 us
    psum x1 -> x0, waiting for transfers between devices: 47.1 us -> none  [per_device(): qkv_weight_grad, out_weight_grad = lax.psum((part_qkv, part_out), 'seq')]
    all_gather x2 -> x3, waiting for transfers between devices: 123 us -> 96.9 us  [the longest x1 49.2 us: per_device(): lax.all_gather(jnp.concatenate([qkv_mine, out_mine], axis=1), 'dp', axis=...]
    unnamed x22 -> x53, local copies, waits for them, and re-layouts: 5.35 us -> 18.7 us
    another operation x0 -> x8, other arithmetic: none -> 12.7 us
    slice x8 -> x10, local copies, waits for them, and re-layouts: 3.09 us -> 15 us  [the longest x2 3.46 us: fold(): total = total.at[:, 1:, :AHEAD].add(value[:, :-1, LEFT + BLOCK:])]
    reshape x2 -> x7, local copies, waits for them, and re-layouts: 4.13 us -> 11.3 us  [the longest x3 6.57 us: per_device(): full = full.transpose(1, 2, 0, 3).reshape(shard_rows, 4 * model_width)]
  transfers between devices with their start and end apart: 9 -> 8, of which waited for: 6 -> 7; matrix products, arithmetic and copies ran while one was open for 14% -> 12% of each run, Pallas kernels for 0% -> 0%
where the time goes in v1:
time: 378 us; the launch traced here: 377 us
  waiting for transfers between devices  222 us (59%)
  local copies, waits for them, and re-layouts  62.1 us (16%)
  matrix products  38.7 us (10%)
  other arithmetic  31.8 us (8%)
  between operations  14.7 us (4%)
  starting transfers between devices  7.41 us (2%)
    unnamed x7, waiting for transfers between devices  57.7 us
    all_gather x1, waiting for transfers between devices, per_device(): lax.all_gather(jnp.concatenate([qkv_mine, out_mine], axis=1), 'dp', axis=...  49.2 us
    all_gather x1, waiting for transfers between devices, per_device(): lax.all_gather(jnp.stack([frames, cotangent]), 'seq', axis=2, tiled=True)  32.9 us
    reduce_scatter x1, waiting for transfers between devices, per_device(): result = lax.psum_scatter(partial, 'seq', scatter_dimension=1, tiled=True)  32.5 us
    reduce_scatter x1, waiting for transfers between devices, per_device(): lax.psum_scatter(norm_part, 'seq', scatter_dimension=1, tiled=True)  30.7 us
    unnamed x53, local copies, waits for them, and re-layouts  18.7 us
    all_gather x1, waiting for transfers between devices, per_device(): full = lax.all_gather(part, 'seq', axis=0)  14.7 us
  transfers between devices with their start and end apart: 8, of which 7 were waited for; matrix products, arithmetic and copies ran while one was open for 12% of the time, Pallas kernels for 0%

profile of v1, /device:TPU:0, one launch (start us, length us, event | category | flops | bytes accessed | tf_op | source)
XLA Modules:
  0.0 376.6 jit_solution(8408538416053653202)
XLA Ops:
  15.6 49.2 %all-gather.7.cloned.1.call-done = bf16[1024,1024]{0,1:T(8,128)(2,1)} async-done(((bf16[128,1024]{0,1:T(8,128)(2,1)}), bf16[1024,1024]{0,1:T(8,128)(2,1)}) %all-gather.7.cloned.1.call-update) | async-done | bytes 2097168 | tf_op jit(solution)/shard_map/all_gather | solution.py:92
  66.7 3.5 all-to-all-start
  70.2 32.9 %all-gather.5.cloned.1.call-done = bf16[2,2,512,1024]{3,2,1,0:T(8,128)(2,1)} async-done(((bf16[2,2,128,1024]{3,2,1,0:T(8,128)(2,1)}), bf16[2,2,512,1024]{3,2,1,0:T(8,128)(2,1)}) %all-gather.5.cloned.1.call-update) | async-done | bytes 4194320 | tf_op jit(solution)/shard_map/all_gather | solution.py:95
  105.2 2.3 fusion.3
  114.7 2.9 reshape.1049
  119.4 4.0 %fusion.49 = (bf16[2,1,196,4,64]{2,0,4,3,1:T(2,128)(2,1)S(1)}, bf16[2,1,196,4,64]{2,0,4,3,1:T(2,128)(2,1)S(1)}, bf16[2,1,196,4,64]{2,0,4,3,1:T(2,128)(2,1)S(1)},...) fusion(bf16[2,512,4,64]{1,0,3,2:T(2,128)(2,1)S(1)} %get-tuple-e, ...), kind=kLoop, calls=%fused_computation.77 | loop fusion | bytes 3702784 | tf_op jit(solution)/shard_map/stack | solution.py:117
  126.4 2.3 convolution_convert_fusion.6
  129.7 3.3 pad_maximum_fusion.4
  133.2 2.2 reshape_squeeze.3
  135.4 2.8 fusion.71
  139.3 2.8 fusion.70
  142.0 6.8 %fusion.30 = bf16[8,128,4,64]{1,3,2,0:T(8,128)(2,1)} fusion(bf16[8,196,4,64]{1,3,2,0:T(8,128)(2,1)S(1)} %bitcast.116, f32[8,4,128,196]{2,3,1,0:T(8,128)} %fusion.71, f32[8,4,128,196]{2,3,1,0:T(8,128)} %get-tuple-element.81, f32[8,4,128]{2,1,0:T(4,128)S(1)} %get-tuple-element.80), kind=kOutput, calls=%fused_computation.45 | convolution fusion | flops 108646592 | bytes 7766016 | tf_op jit(solution)/shard_map/bhfk,bkhe->bfhe/dot_general | solution.py:65
  148.9 7.5 %fusion.11 = f32[8,4,64,196]{3,2,1,0:T(8,128)} fusion(f32[8,4,128,196]{2,3,1,0:T(8,128)} %fusion.71, bf16[8,128,4,64]{1,0,3,2:T(8,128)(2,1)} %reshape_squeeze.3, f32[8,4,128,196]{2,3,1,0:T(8,128)} %get-tuple-element.81, f32[8,4,128]{2,1,0:T(4,128)S(1)} %get-tuple-element.80), kind=kOutput, calls=%fused_computation.17 | convolution fusion | flops 108384448 | bytes 8568832 | tf_op jit(solution)/shard_map/bhfk,bfhe->bkhe/dot_general | solution.py:68
  156.3 3.0 slice.245
  159.4 2.1 slice.246
  161.5 2.3 slice.248
  173.2 2.8 add_select_fusion.1
  176.0 2.7 scatter-add.14
  190.5 2.3 convolution_convert_fusion.5
  193.8 3.5 all-to-all-start.1
  197.5 4.3 %convolution_convert_fusion.2 = bf16[1024,768]{0,1:T(8,128)(2,1)} fusion(bf16[1024,1024]{1,0:T(8,128)(2,1)S(1)} %copy-done.6, bf16[1024,256]{0,1:T(8,128)(2,1)} %copy.80, bf16[1024,256]{0,1:T(8,128)(2,1)} %copy.79, bf16[1024,256]{0,1:T(8,128)(2,1)} %bitcast.139), kind=kOutput, calls=%fused_computation.21 | convolution fusion | flops 1616117760 | bytes 5242880 | tf_op jit(solution)/shard_map/dot_general | solution.py:168
  201.8 4.2 %all-to-all-done.1 = bf16[4,256,256]{1,2,0:T(8,128)(2,1)S(1)} async-done(((bf16[4,256,256]{1,2,0:T(8,128)(2,1)}), bf16[4,256,256]{1,2,0:T(8,128)(2,1)S(1)}, u32[]{:S(2)}, u32[]{:S(2)}) %all-to-all-start.1) | async-done | bytes 524320 | tf_op jit(solution)/shard_map/all_to_all | solution.py:165
  207.8 2.6 copy.85
  210.5 5.0 %convolution_convert_fusion.1 = bf16[1024,1024]{1,0:T(8,128)(2,1)} fusion(bf16[1024,1024]{0,1:T(8,128)(2,1)} %all-gather.7.cloned.1.call-done, bf16[1024,256]{0,1:T(8,128)(2,1)} %copy.80, bf16[1024,256]{0,1:T(8,128)(2,1)} %copy.79, bf16[1024,256]{0,1:T(8,128)(2,1)S(1)} %bitcast.140), kind=kOutput, calls=%fused_computation.20 | convolution fusion | flops 1616379904 | bytes 5242880 | tf_op jit(solution)/shard_map/dot_general | solution.py:156
  215.5 2.1 convolution_convert_fusion
  217.9 57.6 %reduce-scatter.10.cloned.1.call-done = bf16[128,1024]{1,0:T(8,128)(2,1)} async-done(((bf16[1024,1024]{1,0:T(8,128)(2,1)}), bf16[128,1024]{1,0:T(8,128)(2,1)}) %reduce-scatter.10.cloned.1.call-update) | async-done | bytes 262160
  277.6 30.7 %reduce-scatter.8.cloned.1.call-done = bf16[2,128,1024]{2,1,0:T(8,128)(2,1)} async-done(((bf16[2,512,1024]{2,1,0:T(8,128)(2,1)}), bf16[2,128,1024]{2,1,0:T(8,128)(2,1)}) %reduce-scatter.8.cloned.1.call-update) | async-done | bytes 524304 | tf_op jit(solution)/shard_map/reduce_scatter | solution.py:160
  309.7 32.5 %reduce-scatter.6.cloned.1.call-done = bf16[2,128,1024]{2,1,0:T(8,128)(2,1)} async-done(((bf16[2,512,1024]{2,1,0:T(8,128)(2,1)}), bf16[2,128,1024]{2,1,0:T(8,128)(2,1)}) %reduce-scatter.6.cloned.1.call-update) | async-done | bytes 524304 | tf_op jit(solution)/shard_map/reduce_scatter | solution.py:132
  344.2 2.2 fusion.36
  346.4 14.7 %all-gather.9.cloned.1.call-done = bf16[512,1024]{0,1:T(8,128)(2,1)} async-done(((bf16[128,1024]{0,1:T(8,128)(2,1)}), bf16[512,1024]{0,1:T(8,128)(2,1)}) %all-gather.9.cloned.1.call-update) | async-done | bytes 1048592 | tf_op jit(solution)/shard_map/all_gather | solution.py:173
  362.9 2.5 copy.83
  365.3 2.4 reshape.1068
  (139 shorter events, 60.1 us)
Async XLA Ops:
  7.2 1.3 copy-start
  7.2 5.6 %copy-start.18 = (s32[4]{0:T(128)S(1)}, s32[4]{0:T(128)}, u32[]{:S(2)}) copy-start(s32[4]{0:T(128)} %constant.206.clone.1) | copy-start | bytes 52
  7.2 3.7 copy-start.3
  7.2 3.7 copy-start.14
  7.2 6.4 %copy-start.17 = (s32[2]{0:T(128)S(1)}, s32[2]{0:T(128)}, u32[]{:S(2)}) copy-start(s32[2]{0:T(128)} %param.14) | copy-start | bytes 28
  7.2 57.6 %all-gather.7.cloned.1.call-start = ((), (), s32[]{:S(2)}) async-start(), calls=%async_computation.6 | async-start | bytes 2359296 | tf_op jit(solution)/shard_map/all_gather | solution.py:92
  10.9 92.3 %all-gather.5.cloned.1.call-start = ((), (), s32[]{:S(2)}) async-start(), calls=%async_computation.5 | async-start | bytes 5242880 | tf_op jit(solution)/shard_map/all_gather | solution.py:95
  66.7 58.9 %all-to-all-start = ((bf16[4,256,256]{1,2,0:T(8,128)(2,1)}), bf16[4,256,256]{1,2,0:T(8,128)(2,1)S(1)}, u32[]{:S(2)}, u32[]{:S(2)}) async-start(bf16[4,256,256]{1,2,0:T(8,128)(2,1)} %bitcast.109), calls=%async_computation | async-start | bytes 1048576 | tf_op jit(solution)/shard_map/all_to_all | solution.py:99
  103.1 4.4 %copy-start.2 = (bf16[2,2,512,1024]{3,2,1,0:T(8,128)(2,1)S(1)}, bf16[2,2,512,1024]{3,2,1,0:T(8,128)(2,1)}, u32[]{:S(2)}) copy-start(bf16[2,2,512,1024]{3,2,1,0:T(8,128)(2,1)} %all-gather.5.cloned.1.call-done) | copy-start | bytes 12582916
  109.2 2.0 copy-start.16
  109.7 1.4 copy-start.5
  125.6 0.8 copy-start.7
  135.4 2.8 copy-start.4
  138.2 1.1 copy-start.15
  156.3 7.5 %copy-start.19 = (f32[8,4,128,196]{2,3,1,0:T(8,128)S(1)}, f32[8,4,128,196]{2,3,1,0:T(8,128)}, u32[]{:S(2)}) copy-start(f32[8,4,128,196]{2,3,1,0:T(8,128)} %get-tuple-element.81) | copy-start | bytes 9633796
  167.4 1.6 copy-start.13
  181.5 7.8 %copy-start.12 = (bf16[8,128,4,64]{1,3,2,0:T(8,128)(2,1)S(1)}, bf16[8,128,4,64]{1,3,2,0:T(8,128)(2,1)}, u32[]{:S(2)}) copy-start(bf16[8,128,4,64]{1,3,2,0:T(8,128)(2,1)} %fusion.29) | copy-start | bytes 1572868
  189.3 8.2 %copy-start.6 = (bf16[1024,1024]{1,0:T(8,128)(2,1)S(1)}, bf16[1024,1024]{1,0:T(8,128)(2,1)}, u32[]{:S(2)}) copy-start(bf16[1024,1024]{1,0:T(8,128)(2,1)} %copy-done.5) | copy-start | bytes 6291460
  189.7 0.8 copy-start.9
  193.8 12.3 %all-to-all-start.1 = ((bf16[4,256,256]{1,2,0:T(8,128)(2,1)}), bf16[4,256,256]{1,2,0:T(8,128)(2,1)S(1)}, u32[]{:S(2)}, u32[]{:S(2)}) async-start(bf16[4,256,256]{1,2,0:T(8,128)(2,1)} %bitcast.127), calls=%async_computation.3 | async-start | bytes 1048576 | tf_op jit(solution)/shard_map/all_to_all | solution.py:165
  197.3 78.2 %reduce-scatter.10.cloned.1.call-start = ((), (), s32[]{:S(2)}) async-start(), calls=%async_computation.10 | async-start | bytes 2359296
  207.8 2.7 copy-start.11
  210.4 5.1 %copy-start.8 = (bf16[4,256,256]{1,2,0:T(8,128)(2,1)S(1)}, bf16[4,256,256]{1,2,0:T(8,128)(2,1)}, u32[]{:S(2)}) copy-start(bf16[4,256,256]{1,2,0:T(8,128)(2,1)} %copy-done.7) | copy-start | bytes 1572868
  210.4 5.1 %copy-start.10 = (bf16[8,128,4,64]{1,0,3,2:T(8,128)(2,1)S(1)}, bf16[8,128,4,64]{1,0,3,2:T(8,128)(2,1)}, u32[]{:S(2)}) copy-start(bf16[8,128,4,64]{1,0,3,2:T(8,128)(2,1)} %copy-done.9) | copy-start | bytes 1572868
  210.4 97.9 %reduce-scatter.8.cloned.1.call-start = ((), (), s32[]{:S(2)}) async-start(), calls=%async_computation.8 | async-start | bytes 2621440 | tf_op jit(solution)/shard_map/reduce_scatter | solution.py:160
  215.5 126.8 %reduce-scatter.6.cloned.1.call-start = ((), (), s32[]{:S(2)}) async-start(), calls=%async_computation.7 | async-start | bytes 2621440 | tf_op jit(solution)/shard_map/reduce_scatter | solution.py:132
  217.7 143.4 %all-gather.9.cloned.1.call-start = ((), (), s32[]{:S(2)}) async-start(), calls=%async_computation.9 | async-start | bytes 1310720 | tf_op jit(solution)/shard_map/all_gather | solution.py:173
  365.3 4.5 %copy-start.1 = (bf16[128,1024]{1,0:T(8,128)(2,1)S(1)}, bf16[128,1024]{1,0:T(8,128)(2,1)}, u32[]{:S(2)}) copy-start(bf16[128,1024]{1,0:T(8,128)(2,1)} %param.16) | copy-start | bytes 786436
Sparse Core Ops, SparseCore 0:
  11.0 53.8 all-gather.6
  67.0 36.0 all-gather.4
  210.5 64.9 reduce-scatter.9
  277.9 30.3 reduce-scatter.7
  310.8 31.3 reduce-scatter.5
  344.2 16.8 all-gather.8

commit v2 on v1

v2 whole, which is shorter than its diff:
```python
import functools
import math

import jax
import jax.numpy as jnp
from jax import lax
from jax.experimental import pallas as pl
from jax.experimental.pallas import tpu as pltpu
from jax.sharding import PartitionSpec as P

H = 16
GROUP = 16
LEFT = 64
AHEAD = 4
BLOCK = 128
PAD = 64
SPAN = BLOCK + 2 * PAD
MESH = pl.DeviceIdType.MESH
BF = jnp.bfloat16
F32 = jnp.float32
VMEM_LIMIT = 60 * 1024 * 1024


def norm_rows(frames):
    as_float = frames.astype(jnp.float32)
    row_mean = jnp.mean(as_float, axis=-1, keepdims=True)
    centred = as_float - row_mean
    variance = jnp.mean(centred * centred, axis=-1, keepdims=True)
    inv_std = lax.rsqrt(variance + 1e-05)
    return (centred * inv_std, inv_std)


def greet(seq_size, dp_size):
    s, j = lax.axis_index("seq"), lax.axis_index("dp")
    barrier = pltpu.get_barrier_semaphore()
    for d in range(1, seq_size):
        pl.semaphore_signal(
            barrier, inc=1, device_id=(j, lax.rem(s + d, seq_size)), device_id_type=MESH
        )
    for d in range(1, dp_size):
        pl.semaphore_signal(
            barrier, inc=1, device_id=(lax.rem(j + d, dp_size), s), device_id_type=MESH
        )
    pl.semaphore_wait(barrier, seq_size + dp_size - 2)


def gather_kernel(
    seq_size, dp_size, fr, ct, wq, wo, fr_all, ct_all, wq_all, wo_all, wo_mine,
    act_send, act_recv, w_send, w_recv, x_send, x_recv, own_sem,
):
    s, j = lax.axis_index("seq"), lax.axis_index("dp")
    frame_count, shard = fr.shape[1], wq.shape[0]
    wide = wo.shape[1]
    outer, core = s // 2, lax.rem(s, 2)
    outers = seq_size // 2
    zed, why = j // 2, lax.rem(j, 2)
    zeds = dp_size // 2
    greet(seq_size, dp_size)

    def act(k, src, dst_all, owner, to, slot, own):
        place = dst_all.at[:, pl.ds(owner * frame_count, frame_count)]
        return pltpu.make_async_remote_copy(
            src_ref=src if own else place, dst_ref=place,
            send_sem=act_send.at[k, slot], recv_sem=act_recv.at[k, slot],
            device_id=(j, to), device_id_type=MESH,
        )

    def weight(k, src, dst_all, owner, to, slot, own):
        place = dst_all.at[pl.ds(owner * shard, shard)]
        return pltpu.make_async_remote_copy(
            src_ref=src if own else place, dst_ref=place,
            send_sem=w_send.at[k, slot], recv_sem=w_recv.at[k, slot],
            device_id=(to, s), device_id_type=MESH,
        )

    acts = ((fr, fr_all), (ct, ct_all))
    ws = ((wo, wo_all), (wq, wq_all))
    across, beside, started = {}, [], []
    for k, (src, dst) in enumerate(ws):
        for d in range(1, zeds):
            c = weight(k, src, dst, j, lax.rem(zed + d, zeds) * 2 + why, d, True)
            c.start()
            across["w", k, d] = c
    for k, (src, dst) in enumerate(acts):
        for d in range(1, outers):
            c = act(k, src, dst, s, lax.rem(outer + d, outers) * 2 + core, d, True)
            c.start()
            across["a", k, d] = c
    for k, (src, dst) in enumerate(ws):
        c = weight(k, src, dst, j, zed * 2 + 1 - why, 0, True)
        c.start()
        beside.append(c)
    for k, (src, dst) in enumerate(acts):
        c = act(k, src, dst, s, outer * 2 + 1 - core, 0, True)
        c.start()
        beside.append(c)
    local = [
        pltpu.make_async_copy(fr, fr_all.at[:, pl.ds(s * frame_count, frame_count)], own_sem.at[0]),
        pltpu.make_async_copy(ct, ct_all.at[:, pl.ds(s * frame_count, frame_count)], own_sem.at[1]),
        pltpu.make_async_copy(wq, wq_all.at[pl.ds(j * shard, shard)], own_sem.at[2]),
        pltpu.make_async_copy(wo, wo_all.at[pl.ds(j * shard, shard)], own_sem.at[3]),
    ]
    for c in local:
        c.start()

    def forward_w(k, dst, d):
        across["w", k, d].wait_recv()
        owner = lax.rem(zed + zeds - d, zeds) * 2 + why
        c = weight(k, None, dst, owner, zed * 2 + 1 - why, zeds + d, False)
        c.start()
        return c

    def forward_a(k, dst, d):
        across["a", k, d].wait_recv()
        owner = lax.rem(outer + outers - d, outers) * 2 + core
        c = act(k, None, dst, owner, outer * 2 + 1 - core, outers + d, False)
        c.start()
        return c

    near_out = [forward_w(0, wo_all, d) for d in range(1, zeds)]
    late = [forward_w(1, wq_all, d) for d in range(1, zeds)]
    late += [forward_a(0, fr_all, d) for d in range(1, outers)]
    late += [forward_a(1, ct_all, d) for d in range(1, outers)]
    local[3].wait()
    for c in [beside[0]] + near_out:
        c.wait_recv()
    swaps = []
    for d in range(1, seq_size):
        to = lax.rem(s + d, seq_size)
        c = pltpu.make_async_remote_copy(
            src_ref=wo_all.at[pl.ds(to * wide, wide)], dst_ref=wo_mine.at[s],
            send_sem=x_send.at[d], recv_sem=x_recv.at[d],
            device_id=(j, to), device_id_type=MESH,
        )
        c.start()
        swaps.append(c)
    last = pltpu.make_async_copy(wo_all.at[pl.ds(s * wide, wide)], wo_mine.at[s], own_sem.at[4])
    last.start()
    for c in beside[1:] + late:
        c.wait_recv()
    for c in swaps:
        c.wait_recv()
    for c in list(across.values()) + beside + near_out + late + swaps:
        c.wait_send()
    for c in local[:3] + [last]:
        c.wait()


def gather(frames, cotangent, wq, wo):
    seq_size, dp_size = lax.axis_size("seq"), lax.axis_size("dp")
    records, frame_count, width = frames.shape
    shard, wide = wo.shape
    anywhere = pl.BlockSpec(memory_space=pl.ANY)
    slab = jax.ShapeDtypeStruct((records, frame_count * seq_size, width), BF)
    dma = pltpu.SemaphoreType.DMA
    return pl.pallas_call(
        functools.partial(gather_kernel, seq_size, dp_size),
        out_shape=(
            slab, slab,
            jax.ShapeDtypeStruct((shard * dp_size, 3 * wide), BF),
            jax.ShapeDtypeStruct((shard * dp_size, wide), BF),
            jax.ShapeDtypeStruct((seq_size, wide, wide), BF),
        ),
        in_specs=[anywhere] * 4,
        out_specs=(anywhere,) * 5,
        scratch_shapes=[
            dma((2, seq_size)), dma((2, seq_size)), dma((2, dp_size)), dma((2, dp_size)),
            dma((seq_size,)), dma((seq_size,)), dma((5,)),
        ],
        compiler_params=pltpu.CompilerParams(collective_id=0, has_side_effects=True),
    )(frames, cotangent, wq, wo)


def dot(a, b, ca=1, cb=0):
    return lax.dot_general(a, b, (((ca,), (cb,)), ((), ())), preferred_element_type=F32)


def core_kernel(
    head_size, lengths, fr, ct, wq, wo, result, norm_part, wq_part, wo_part,
    normed, og, qkv, mgrad, mixed, kv_acc, qkv_grad, wq_acc, wo_acc,
):
    rec = pl.program_id(0)
    slab, width = fr.shape[1:]
    wide = wo.shape[0]
    length = lengths[rec]
    scale = 1.0 / math.sqrt(head_size)
    chunk = min(512, slab)
    pair = min(wide, 128)
    per = pair // head_size
    pad_zero = jnp.zeros((PAD, 3 * wide), BF)
    qkv[pl.ds(0, PAD), :] = pad_zero
    qkv[pl.ds(PAD + slab, PAD), :] = pad_zero
    kv_acc[...] = jnp.zeros_like(kv_acc)

    @pl.when(rec == 0)
    def _():
        wq_acc[...] = jnp.zeros_like(wq_acc)
        wo_acc[...] = jnp.zeros_like(wo_acc)

    @pl.loop(0, slab // BLOCK)
    def _(b):
        rows = pl.ds(pl.multiple_of(b * BLOCK, BLOCK), BLOCK)
        normed[rows, :] = norm_rows(fr[0, rows, :])[0].astype(BF)
        pos = b * BLOCK + lax.broadcasted_iota(jnp.int32, (BLOCK, width), 0)
        og[rows, :] = jnp.where(pos < length, ct[0, rows, :].astype(F32), 0.0).astype(BF)

    @pl.loop(0, slab // chunk)
    def _(b):
        start = pl.multiple_of(b * chunk, chunk)
        rows = pl.ds(start, chunk)
        qkv[pl.ds(PAD + start, chunk), :] = dot(normed[rows, :], wq[...]).astype(BF)
        mgrad[rows, :] = dot(og[rows, :], wo[...], 1, 1).astype(BF)

    @pl.loop(0, slab // BLOCK)
    def _(b):
        start = pl.multiple_of(b * BLOCK, BLOCK)
        rows = pl.ds(start, BLOCK)
        window = pl.ds(start, SPAN)
        shape = (per * BLOCK, SPAN)
        t = start + lax.rem(lax.broadcasted_iota(jnp.int32, shape, 0), BLOCK)
        k = start - PAD + lax.broadcasted_iota(jnp.int32, shape, 1)
        c = t - lax.rem(t, GROUP)
        allowed = (k >= 0) & (k < slab) & (k >= c - LEFT) & (k < c + GROUP + AHEAD)
        allowed = allowed & ((k < length) | (t >= length))
        lane = lax.broadcasted_iota(jnp.int32, (BLOCK, pair), 1) // head_size

        def stack(value):
            if per == 1:
                return value
            value = value.astype(F32)
            return jnp.concatenate(
                [jnp.where(lane == i, value, 0.0) for i in range(per)], axis=0
            ).astype(BF)

        def unstack(value):
            out = value[:BLOCK]
            for i in range(1, per):
                out = jnp.where(lane == i, value[i * BLOCK : (i + 1) * BLOCK], out)
            return out

        for p in range(wide // pair):
            cols = pl.ds(p * pair, pair)
            kcols = pl.ds(wide + p * pair, pair)
            vcols = pl.ds(2 * wide + p * pair, pair)
            q = stack(qkv[pl.ds(PAD + start, BLOCK), cols])
            mg = stack(mgrad[rows, cols])
            keys = qkv[window, kcols]
            values = qkv[window, vcols]
            scores = jnp.where(allowed, dot(q, keys, 1, 1) * scale, -1e30)
            shifted = jnp.exp(scores - jnp.max(scores, axis=-1, keepdims=True))
            shifted = jnp.where(allowed, shifted, 0.0)
            probs = shifted / jnp.sum(shifted, axis=-1, keepdims=True)
            half = probs.astype(BF)
            mixed[rows, cols] = unstack(dot(half, values)).astype(BF)
            pg = dot(mg, values, 1, 1)
            sg = probs * (pg - jnp.sum(probs * pg, axis=-1, keepdims=True)) * scale
            sg = sg.astype(BF)
            qkv_grad[rows, cols] = unstack(dot(sg, keys)).astype(BF)
            kv_acc[window, cols] += dot(sg, q, 0, 0)
            kv_acc[window, kcols] += dot(half, mg, 0, 0)

    @pl.loop(0, slab // chunk)
    def _(b):
        start = pl.multiple_of(b * chunk, chunk)
        rows = pl.ds(start, chunk)
        qkv_grad[rows, pl.ds(wide, 2 * wide)] = kv_acc[pl.ds(PAD + start, chunk), :].astype(BF)
        pos = start + lax.broadcasted_iota(jnp.int32, (chunk, width), 0)
        out = jnp.where(pos < length, dot(mixed[rows, :], wo[...]), 0.0)
        result[0, rows, :] = out.astype(BF)
        norm_part[0, rows, :] = dot(qkv_grad[rows, :], wq[...], 1, 1).astype(BF)
        wq_acc[...] += dot(normed[rows, :], qkv_grad[rows, :], 0, 0)
        wo_acc[...] += dot(mixed[rows, :], og[rows, :], 0, 0)

    @pl.when(rec == pl.num_programs(0) - 1)
    def _():
        wq_part[...] = wq_acc[...].astype(BF)
        wo_part[...] = wo_acc[...].astype(BF)


def core(lengths, fr_all, ct_all, wq_all, wo_rows):
    records, slab, width = fr_all.shape
    wide = wo_rows.shape[0]
    per_rec = pl.BlockSpec((1, slab, width), lambda r: (r, 0, 0))
    wq_spec = pl.BlockSpec((width, 3 * wide), lambda r: (0, 0))
    wo_spec = pl.BlockSpec((wide, width), lambda r: (0, 0))
    rows = jax.ShapeDtypeStruct((records, slab, width), BF)
    return pl.pallas_call(
        functools.partial(core_kernel, width // H),
        grid=(records,),
        out_shape=(
            rows, rows,
            jax.ShapeDtypeStruct((width, 3 * wide), BF),
            jax.ShapeDtypeStruct((wide, width), BF),
        ),
        in_specs=[pl.BlockSpec(memory_space=pltpu.SMEM), per_rec, per_rec, wq_spec, wo_spec],
        out_specs=(per_rec, per_rec, wq_spec, wo_spec),
        scratch_shapes=[
            pltpu.VMEM((slab, width), BF),
            pltpu.VMEM((slab, width), BF),
            pltpu.VMEM((slab + 2 * PAD, 3 * wide), BF),
            pltpu.VMEM((slab, wide), BF),
            pltpu.VMEM((slab, wide), BF),
            pltpu.VMEM((slab + 2 * PAD, 2 * wide), F32),
            pltpu.VMEM((slab, 3 * wide), BF),
            pltpu.VMEM((width, 3 * wide), F32),
            pltpu.VMEM((wide, width), F32),
        ],
        compiler_params=pltpu.CompilerParams(vmem_limit_bytes=VMEM_LIMIT),
    )(lengths, fr_all, ct_all, wq_all, wo_rows)


def per_device(frames, lengths, qkv_weight, out_weight, cotangent):
    records, frame_count, model_width = frames.shape
    seq_size = lax.axis_size("seq")
    seq_index = lax.axis_index("seq")
    wide = model_width // seq_size
    shard_rows = qkv_weight.shape[0]
    qkv_mine = lax.dynamic_index_in_dim(
        qkv_weight.reshape(shard_rows, 3, seq_size, wide), seq_index, 2, False
    ).reshape(shard_rows, 3 * wide)
    out_mine = lax.dynamic_slice_in_dim(out_weight, seq_index * wide, wide, 1)
    fr_all, ct_all, wq_all, _, wo_mine = gather(frames, cotangent, qkv_mine, out_mine)
    wo_rows = jnp.swapaxes(wo_mine, 0, 1).reshape(wide, model_width)
    partial, norm_part, part_qkv, part_out = core(lengths, fr_all, ct_all, wq_all, wo_rows)
    return finish(frames, partial, norm_part, part_qkv, part_out, shard_rows)


def finish(frames, partial, norm_part, part_qkv, part_out, shard_rows):
    model_width = frames.shape[-1]
    seq_size = lax.axis_size("seq")
    wide = model_width // seq_size
    result = lax.psum_scatter(partial, "seq", scatter_dimension=1, tiled=True)
    norm_grad = lax.psum_scatter(norm_part, "seq", scatter_dimension=1, tiled=True)
    norm_grad = norm_grad.astype(F32)
    part_out = lax.all_to_all(
        jnp.swapaxes(part_out.reshape(wide, seq_size, wide), 0, 1), "seq", 0, 0
    ).reshape(model_width, wide)
    part = jnp.concatenate([part_qkv, part_out], axis=1)
    part = lax.psum_scatter(part, "dp", scatter_dimension=0, tiled=True)
    full = lax.all_gather(part, "seq", axis=0)
    full = full.reshape(seq_size, shard_rows, 4, wide).astype(F32)
    full = full.transpose(1, 2, 0, 3).reshape(shard_rows, 4 * model_width)
    qkv_weight_grad = full[:, : 3 * model_width]
    out_weight_grad = full[:, 3 * model_width :]
    centred, inv_std = norm_rows(frames)
    mean_one = jnp.mean(norm_grad, axis=-1, keepdims=True)
    mean_two = jnp.mean(norm_grad * centred, axis=-1, keepdims=True)
    frame_grad = ((norm_grad - mean_one - centred * mean_two) * inv_std).astype(BF)
    return (result, frame_grad, qkv_weight_grad, out_weight_grad)


def solution(mesh):
    in_specs = (P("dp", "seq", None), P("dp"), P("dp", None), P("dp", None), P("dp", "seq", None))
    out_specs = (P("dp", "seq", None), P("dp", "seq", None), P("dp", None), P("dp", None))
    return jax.shard_map(
        per_device, mesh=mesh, in_specs=in_specs, out_specs=out_specs, check_vma=False
    )
```

time: 378 us -> 266 us (0.70)
  waiting for transfers between devices: 222 us -> 138 us
  Pallas kernels: 0 us -> 80.7 us
  local copies, waits for them, and re-layouts: 62.1 us -> 15.2 us
  matrix products: 38.7 us -> 0 us
  other arithmetic: 31.8 us -> 5.74 us
  blocking collectives: 0 us -> 11.5 us
  starting transfers between devices: 7.41 us -> 0.16 us
    all_gather x3 -> x1, waiting for transfers between devices: 96.9 us -> 14.7 us  [finish(): full = lax.all_gather(part, 'seq', axis=0)]
    pallas_call x0 -> x2, Pallas kernels: none -> 80.7 us  [the longest x1 53.6 us: gather(): pl.pallas_call(functools.partial(gather_kernel, seq_size, dp_size), out_s...]
    reduce_scatter x2 -> x3, waiting for transfers between devices: 63.2 us -> 122 us  [the longest x1 65 us: finish(): part = lax.psum_scatter(part, 'dp', scatter_dimension=0, tiled=True)]
    unnamed x7 -> x4, waiting for transfers between devices: 57.7 us -> 1.24 us
    dot_general x12 -> x0, matrix products: 38.7 us -> none  [the longest x1 7.46 us: attend_back(): jnp.einsum('bhfk,bfhe->bkhe', score_grad, queries, preferred_element_type...]
    unnamed x53 -> x7, local copies, waits for them, and re-layouts: 18.7 us -> 1.56 us
    slice x10 -> x2, local copies, waits for them, and re-layouts: 15 us -> 2.08 us  [the longest x1 1.25 us: finish(): qkv_weight_grad = full[:, :3 * model_width]]
    another operation x8 -> x0, other arithmetic: 12.7 us -> none
  transfers between devices with their start and end apart: 8 -> 4, of which waited for: 7 -> 4; matrix products, arithmetic and copies ran while one was open for 12% -> 5% of each run, Pallas kernels for 0% -> 0%
where the time goes in v2:
time: 266 us
  waiting for transfers between devices  138 us (52%)
  Pallas kernels  80.7 us (30%)
  local copies, waits for them, and re-layouts  15.2 us (6%)
  between operations  13.9 us (5%)
  blocking collectives  11.5 us (4%)
  other arithmetic  5.74 us (2%)
    reduce_scatter x1, waiting for transfers between devices, finish(): part = lax.psum_scatter(part, 'dp', scatter_dimension=0, tiled=True)  65 us
    pallas_call x1, Pallas kernels, gather(): pl.pallas_call(functools.partial(gather_kernel, seq_size, dp_size), out_s...  53.6 us
    reduce_scatter x1, waiting for transfers between devices, finish(): lax.psum_scatter(norm_part, 'seq', scatter_dimension=1, tiled=True)  31.9 us
    pallas_call x1, Pallas kernels, core(): pl.pallas_call(functools.partial(core_kernel, width // H), grid=(records,...  27.1 us
    reduce_scatter x1, waiting for transfers between devices, finish(): result = lax.psum_scatter(partial, 'seq', scatter_dimension=1, tiled=True)  25.5 us
    all_gather x1, waiting for transfers between devices, finish(): full = lax.all_gather(part, 'seq', axis=0)  14.7 us
    all_to_all x1, blocking collectives, finish(): lax.all_to_all(jnp.swapaxes(part_out.reshape(wide, seq_size, wide), 0, 1)...  11.5 us
    reshape x3, local copies, waits for them, and re-layouts, finish(): full = full.transpose(1, 2, 0, 3).reshape(shard_rows, 4 * model_width)  6.97 us
  transfers between devices with their start and end apart: 4, of which 4 were waited for; matrix products, arithmetic and copies ran while one was open for 5% of the time, Pallas kernels for 0%

profile of v2, /device:TPU:0, one launch (start us, length us, event | category | flops | bytes accessed | tf_op | source)
XLA Modules:
  0.0 265.6 jit_solution(10498264069395593462)
XLA Ops:
  7.2 0.0 copy-start
  7.2 0.0 reduce-scatter.8.cloned.1.call-start
  7.2 1.5 copy.22
  8.8 0.8 copy.23.wq
  9.6 0.6 constant_dynamic-slice_fusion.wo
  10.3 53.6 %shard_map.84 = (bf16[2,512,1024]{2,1,0:T(8,128)(2,1)}, bf16[2,512,1024]{2,1,0:T(8,128)(2,1)}, bf16[1024,768]{1,0:T(8,128)(2,1)}, bf16[1024,256]{1,0:T(8,128)(2,1)}, bf16[4,256,256]{2,1,0:T(8,128)(2,1)}) custom-call(bf16[2,128,1024]{2,1,0:T(8,128)(2,1)} %fr.1, bf16[2,128,1024]{2,1,0:T(8,128)(2,1)} %ct.1, bf16[128,768]{1,0:T(8,128)(2,1)} %copy.23.wq, ...), custom_call_target="tpu_custom_call" | custom-call | tf_op jit(solution)/shard_map/pallas_call | solution.py:156
  63.9 1.9 copy.28
  65.8 27.1 %shard_map.85 = (bf16[2,512,1024]{2,1,0:T(8,128)(2,1)}, bf16[2,512,1024]{2,1,0:T(8,128)(2,1)}, bf16[1024,768]{1,0:T(8,128)(2,1)}, bf16[256,1024]{1,0:T(8,128)(2,1)}) custom-call(s32[2]{0:T(128)} %lengths.1, bf16[2,512,1024]{2,1,0:T(8,128)(2,1)} %get-tuple-element.12.fr, bf16[2,512,1024]{2,1,0:T(8,128)(2,1)} %get-tuple-element.13.ct, ...), custom_call_target="tpu_custom_call" | custom-call | tf_op jit(solution)/shard_map/pallas_call | solution.py:287
  92.9 0.0 copy-start.2
  92.9 1.2 copy.30
  94.1 11.5 %all_to_all.5 = bf16[4,256,256]{2,1,0:T(8,128)(2,1)S(1)} all-to-all(bf16[4,256,256]{2,1,0:T(8,128)(2,1)S(1)} %bitcast.16), channel_id=1, replica_groups=mesh['dp'=8,'seq'=4] {'seq'}, dimensions={0} | all-to-all | bytes 1048576 | tf_op jit(solution)/shard_map/all_to_all | solution.py:335
  105.6 1.6 pad_maximum_fusion
  107.2 0.0 reduce-scatter.8.cloned.1.call-update
  107.3 0.0 reduce-scatter.6.cloned.1.call-start
  107.3 0.7 reduce-scatter.6.cloned.1.call-update
  108.0 0.0 all-gather.3.cloned.1.call-start
  108.1 65.0 %reduce-scatter.8.cloned.1.call-done = bf16[128,1024]{1,0:T(8,128)(2,1)} async-done(((bf16[1024,1024]{1,0:T(8,128)(2,1)}), bf16[128,1024]{1,0:T(8,128)(2,1)}) %reduce-scatter.8.cloned.1.call-update) | async-done | bytes 262160 | tf_op jit(solution)/shard_map/reduce_scatter | solution.py:339
  173.1 0.0 all-gather.3.cloned.1.call-update
  173.1 0.0 reduce-scatter.4.cloned.1.call-start
  173.2 0.5 reduce-scatter.4.cloned.1.call-update
  173.7 0.1 convert_reduce_fusion.1
  173.9 0.3 fusion.6
  174.2 31.9 %reduce-scatter.6.cloned.1.call-done = bf16[2,128,1024]{2,1,0:T(8,128)(2,1)} async-done(((bf16[2,512,1024]{2,1,0:T(8,128)(2,1)}), bf16[2,128,1024]{2,1,0:T(8,128)(2,1)}) %reduce-scatter.6.cloned.1.call-update) | async-done | bytes 524304 | tf_op jit(solution)/shard_map/reduce_scatter | solution.py:333
  206.1 1.5 convert_reduce_fusion
  207.5 2.2 fusion.5
  209.7 14.7 %all-gather.3.cloned.1.call-done = bf16[512,1024]{1,0:T(8,128)(2,1)} async-done(((bf16[128,1024]{1,0:T(8,128)(2,1)}), bf16[512,1024]{1,0:T(8,128)(2,1)}) %all-gather.3.cloned.1.call-update) | async-done | bytes 1048592 | tf_op jit(solution)/shard_map/all_gather | solution.py:340
  224.5 2.0 reshape.64
  226.5 2.6 copy.26
  229.1 2.3 reshape.61
  231.5 1.3 slice.8
  232.7 0.8 slice.9
  233.5 25.5 %reduce-scatter.4.cloned.1.call-done = bf16[2,128,1024]{2,1,0:T(8,128)(2,1)} async-done(((bf16[2,512,1024]{2,1,0:T(8,128)(2,1)}), bf16[2,128,1024]{2,1,0:T(8,128)(2,1)}) %reduce-scatter.4.cloned.1.call-update) | async-done | bytes 524304 | tf_op jit(solution)/shard_map/reduce_scatter | solution.py:332
  (8 shorter events, 0.1 us)
Async XLA Ops:
  7.2 2.5 copy-start
  7.2 165.9 %reduce-scatter.8.cloned.1.call-start = ((), (), s32[]{:S(2)}) async-start(), calls=%async_computation.6 | async-start | bytes 2359296 | tf_op jit(solution)/shard_map/reduce_scatter | solution.py:339
  92.9 12.7 %copy-start.2 = (bf16[1024,768]{1,0:T(8,128)(2,1)S(1)}, bf16[1024,768]{1,0:T(8,128)(2,1)}, u32[]{:S(2)}) copy-start(bf16[1024,768]{1,0:T(8,128)(2,1)} %get-tuple-element.18) | copy-start | bytes 4718596
  107.3 98.8 %reduce-scatter.6.cloned.1.call-start = ((), (), s32[]{:S(2)}) async-start(), calls=%async_computation.5 | async-start | bytes 2621440 | tf_op jit(solution)/shard_map/reduce_scatter | solution.py:333
  107.3 66.4 %copy-start.1 = (bf16[2,128,1024]{2,1,0:T(8,128)(2,1)S(1)}, bf16[2,128,1024]{2,1,0:T(8,128)(2,1)}, u32[]{:S(2)}) copy-start(bf16[2,128,1024]{2,1,0:T(8,128)(2,1)} %fr.1) | copy-start | bytes 1572868
  108.0 116.4 %all-gather.3.cloned.1.call-start = ((), (), s32[]{:S(2)}) async-start(), calls=%async_computation.7 | async-start | bytes 1310720 | tf_op jit(solution)/shard_map/all_gather | solution.py:340
  173.1 85.9 %reduce-scatter.4.cloned.1.call-start = ((), (), s32[]{:S(2)}) async-start(), calls=%async_computation.4 | async-start | bytes 2621440 | tf_op jit(solution)/shard_map/reduce_scatter | solution.py:332
Sparse Core Ops, SparseCore 0:
  107.4 65.6 reduce-scatter.7
  175.6 30.3 reduce-scatter.5
  207.7 16.7 all-gather.2
  227.6 31.4 reduce-scatter.3

commit v3 on v2

--- a/solution.py
+++ b/solution.py
@@ -274,7 +274,8 @@
     @pl.when(rec == pl.num_programs(0) - 1)
     def _():
         wq_part[...] = wq_acc[...].astype(BF)
-        wo_part[...] = wo_acc[...].astype(BF)
+        for p in range(width // wide):
+            wo_part[p] = wo_acc[:, p * wide : (p + 1) * wide].astype(BF)
 
 
 def core(lengths, fr_all, ct_all, wq_all, wo_rows):
@@ -290,10 +291,13 @@
         out_shape=(
             rows, rows,
             jax.ShapeDtypeStruct((width, 3 * wide), BF),
-            jax.ShapeDtypeStruct((wide, width), BF),
+            jax.ShapeDtypeStruct((width // wide, wide, wide), BF),
         ),
         in_specs=[pl.BlockSpec(memory_space=pltpu.SMEM), per_rec, per_rec, wq_spec, wo_spec],
-        out_specs=(per_rec, per_rec, wq_spec, wo_spec),
+        out_specs=(
+            per_rec, per_rec, wq_spec,
+            pl.BlockSpec((width // wide, wide, wide), lambda r: (0, 0, 0)),
+        ),
         scratch_shapes=[
             pltpu.VMEM((slab, width), BF),
             pltpu.VMEM((slab, width), BF),
@@ -322,31 +326,190 @@
     fr_all, ct_all, wq_all, _, wo_mine = gather(frames, cotangent, qkv_mine, out_mine)
     wo_rows = jnp.swapaxes(wo_mine, 0, 1).reshape(wide, model_width)
     partial, norm_part, part_qkv, part_out = core(lengths, fr_all, ct_all, wq_all, wo_rows)
-    return finish(frames, partial, norm_part, part_qkv, part_out, shard_rows)
-
-
-def finish(frames, partial, norm_part, part_qkv, part_out, shard_rows):
-    model_width = frames.shape[-1]
-    seq_size = lax.axis_size("seq")
-    wide = model_width // seq_size
-    result = lax.psum_scatter(partial, "seq", scatter_dimension=1, tiled=True)
-    norm_grad = lax.psum_scatter(norm_part, "seq", scatter_dimension=1, tiled=True)
-    norm_grad = norm_grad.astype(F32)
-    part_out = lax.all_to_all(
-        jnp.swapaxes(part_out.reshape(wide, seq_size, wide), 0, 1), "seq", 0, 0
-    ).reshape(model_width, wide)
-    part = jnp.concatenate([part_qkv, part_out], axis=1)
-    part = lax.psum_scatter(part, "dp", scatter_dimension=0, tiled=True)
-    full = lax.all_gather(part, "seq", axis=0)
-    full = full.reshape(seq_size, shard_rows, 4, wide).astype(F32)
-    full = full.transpose(1, 2, 0, 3).reshape(shard_rows, 4 * model_width)
-    qkv_weight_grad = full[:, : 3 * model_width]
-    out_weight_grad = full[:, 3 * model_width :]
-    centred, inv_std = norm_rows(frames)
-    mean_one = jnp.mean(norm_grad, axis=-1, keepdims=True)
-    mean_two = jnp.mean(norm_grad * centred, axis=-1, keepdims=True)
-    frame_grad = ((norm_grad - mean_one - centred * mean_two) * inv_std).astype(BF)
-    return (result, frame_grad, qkv_weight_grad, out_weight_grad)
+    return reduce_all(frames, partial, norm_part, part_qkv, part_out, shard_rows)
+
+
+def reduce_kernel(
+    seq_size, dp_size, fr, res_part, norm_part, wq_part, wo_part,
+    result, frame_grad, qkv_out, out_out,
+    wo_cols, near_r, far_r, near_n, far_n, near_q, far_q, near_o, far_o,
+    mine_q, mine_o, got_q, got_o, send_sem, recv_sem, own_sem,
+):
+    s, j = lax.axis_index("seq"), lax.axis_index("dp")
+    records, frame_count, width = fr.shape
+    wide = wo_part.shape[1]
+    shard = qkv_out.shape[0]
+    greet(seq_size, dp_size)
+    every = []
+
+    def start(src, dst, to):
+        n = len(every)
+        c = pltpu.make_async_remote_copy(
+            src_ref=src, dst_ref=dst, send_sem=send_sem.at[n], recv_sem=recv_sem.at[n],
+            device_id=to, device_id_type=MESH,
+        )
+        c.start()
+        every.append(c)
+        return c
+
+    class Hop:
+        def __init__(self, block, near, far, me, size, device):
+            self.block, self.near, self.far = block, near, far
+            self.hi, self.lo, self.his = me // 2, lax.rem(me, 2), size // 2
+            self.device = device
+
+        def first(self):
+            self.coming = {}
+            for d in list(range(1, self.his)) + [0]:
+                owner = lax.rem(self.hi + d, self.his) * 2 + 1 - self.lo
+                self.coming[d] = start(
+                    self.block(owner), self.near.at[d], self.device(self.hi * 2 + 1 - self.lo)
+                )
+
+        def second(self):
+            self.late = []
+            for d in range(1, self.his):
+                self.coming[d].wait_recv()
+                owner = lax.rem(self.hi + d, self.his) * 2 + self.lo
+                own = self.block(owner)
+                each_chunk(self.near.at[d], lambda at: put(
+                    self.near.at[d], at, self.near.at[d][at].astype(F32) + own[at].astype(F32)
+                ))
+                self.late.append(start(self.near.at[d], self.far.at[d], self.device(owner)))
+
+        def wait(self):
+            self.coming[0].wait_recv()
+            for c in self.late:
+                c.wait_recv()
+            self.own = self.block(self.hi * 2 + self.lo)
+
+        def total(self, at):
+            value = self.near.at[0][at].astype(F32) + self.own[at].astype(F32)
+            for d in range(1, self.his):
+                value = value + self.far.at[d][at].astype(F32)
+            return value
+
+    def put(ref, at, value):
+        ref[at] = value.astype(ref.dtype)
+
+    def each_chunk(ref, body):
+        if len(ref.shape) == 3:
+            for r in range(ref.shape[0]):
+                @pl.loop(0, ref.shape[1] // 32)
+                def _(b):
+                    body((r, pl.ds(pl.multiple_of(b * 32, 32), 32)))
+        else:
+            @pl.loop(0, ref.shape[0] // 32)
+            def _(b):
+                body((pl.ds(pl.multiple_of(b * 32, 32), 32),))
+
+    on_dp = lambda i: (i, s)
+    on_seq = lambda i: (j, i)
+    frame_block = lambda ref: lambda i: ref.at[:, pl.ds(i * frame_count, frame_count)]
+    row_block = lambda ref: lambda i: ref.at[pl.ds(i * shard, shard)]
+    hop_q = Hop(row_block(wq_part), near_q, far_q, j, dp_size, on_dp)
+    hop_o = Hop(row_block(wo_cols), near_o, far_o, j, dp_size, on_dp)
+    hop_n = Hop(frame_block(norm_part), near_n, far_n, s, seq_size, on_seq)
+    hop_r = Hop(frame_block(res_part), near_r, far_r, s, seq_size, on_seq)
+
+    swaps = []
+    hop_q.first()
+    for d in range(1, seq_size):
+        to = lax.rem(s + d, seq_size)
+        swaps.append(start(wo_part.at[to], wo_cols.at[pl.ds(s * wide, wide)], on_seq(to)))
+    own = pltpu.make_async_copy(wo_part.at[s], wo_cols.at[pl.ds(s * wide, wide)], own_sem)
+    own.start()
+    hop_n.first()
+    hop_r.first()
+    own.wait()
+    for c in swaps:
+        c.wait_recv()
+    hop_o.first()
+    hop_n.second()
+    hop_q.second()
+    hop_o.second()
+    hop_r.second()
+
+    hop_n.wait()
+
+    def normalise(at):
+        centred, inv_std = norm_rows(fr[at])
+        grad = hop_n.total(at)
+        one = jnp.mean(grad, axis=-1, keepdims=True)
+        two = jnp.mean(grad * centred, axis=-1, keepdims=True)
+        frame_grad[at] = ((grad - one - centred * two) * inv_std).astype(BF)
+
+    each_chunk(fr, normalise)
+
+    hop_q.wait()
+    each_chunk(mine_q, lambda at: put(mine_q, at, hop_q.total(at)))
+    hop_o.wait()
+    each_chunk(mine_o, lambda at: put(mine_o, at, hop_o.total(at)))
+    arrivals = {}
+    for d in range(1, seq_size):
+        to = lax.rem(s + d, seq_size)
+        arrivals[d] = (
+            start(mine_q, got_q.at[s], on_seq(to)), start(mine_o, got_o.at[s], on_seq(to))
+        )
+
+    hop_r.wait()
+    each_chunk(result, lambda at: put(result, at, hop_r.total(at)))
+
+    local = [
+        pltpu.make_async_copy(mine_q, got_q.at[s], own_sem),
+        pltpu.make_async_copy(mine_o, got_o.at[s], own_sem),
+    ]
+    for c in local:
+        c.start()
+        c.wait()
+    for pair in arrivals.values():
+        for c in pair:
+            c.wait_recv()
+    for p in range(seq_size):
+        for k in range(3):
+            qkv_out[:, k * width + p * wide : k * width + (p + 1) * wide] = got_q[
+                p, :, k * wide : (k + 1) * wide
+            ].astype(F32)
+        out_out[:, p * wide : (p + 1) * wide] = got_o[p].astype(F32)
+    for c in every:
+        c.wait_send()
+
+
+def reduce_all(frames, partial, norm_part, part_qkv, part_out, shard):
+    records, frame_count, width = frames.shape
+    seq_size, dp_size = lax.axis_size("seq"), lax.axis_size("dp")
+    wide = width // seq_size
+    vmem = pl.BlockSpec(memory_space=pltpu.VMEM)
+    outers, zeds = seq_size // 2, dp_size // 2
+    act = pltpu.VMEM((outers, records, frame_count, width), BF)
+    wq = pltpu.VMEM((zeds, shard, 3 * wide), BF)
+    wo = pltpu.VMEM((zeds, shard, wide), BF)
+    copies = 4 * (seq_size + dp_size) + 3 * seq_size
+    return pl.pallas_call(
+        functools.partial(reduce_kernel, seq_size, dp_size),
+        out_shape=(
+            jax.ShapeDtypeStruct(frames.shape, BF),
+            jax.ShapeDtypeStruct(frames.shape, BF),
+            jax.ShapeDtypeStruct((shard, 3 * width), F32),
+            jax.ShapeDtypeStruct((shard, width), F32),
+        ),
+        in_specs=[vmem] * 5,
+        out_specs=(vmem,) * 4,
+        scratch_shapes=[
+            pltpu.VMEM((width, wide), BF),
+            act, act, act, act, wq, wq, wo, wo,
+            pltpu.VMEM((shard, 3 * wide), BF),
+            pltpu.VMEM((shard, wide), BF),
+            pltpu.VMEM((seq_size, shard, 3 * wide), BF),
+            pltpu.VMEM((seq_size, shard, wide), BF),
+            pltpu.SemaphoreType.DMA((copies,)),
+            pltpu.SemaphoreType.DMA((copies,)),
+            pltpu.SemaphoreType.DMA,
+        ],
+        compiler_params=pltpu.CompilerParams(
+            collective_id=1, has_side_effects=True, vmem_limit_bytes=VMEM_LIMIT
+        ),
+    )(frames, partial, norm_part, part_qkv, part_out)
 
 
 def solution(mesh):

time: 266 us -> 148 us (0.56)
  waiting for transfers between devices: 138 us -> 0 us
  Pallas kernels: 80.7 us -> 135 us
  between operations: 13.9 us -> 0.69 us
  blocking collectives: 11.5 us -> 0 us
  other arithmetic: 5.74 us -> 0 us
  local copies, waits for them, and re-layouts: 15.2 us -> 11.7 us
    reduce_scatter x3 -> x0, waiting for transfers between devices: 122 us -> none  [the longest x1 65 us: finish(): part = lax.psum_scatter(part, 'dp', scatter_dimension=0, tiled=True)]
    pallas_call x0 -> x1, Pallas kernels: none -> 54 us  [reduce_all(): pl.pallas_call(functools.partial(reduce_kernel, seq_size, dp_size), out_s...]
    all_gather x1 -> x0, waiting for transfers between devices: 14.7 us -> none  [finish(): full = lax.all_gather(part, 'seq', axis=0)]
    all_to_all x1 -> x0, blocking collectives: 11.5 us -> none  [finish(): lax.all_to_all(jnp.swapaxes(part_out.reshape(wide, seq_size, wide), 0, 1)...]
    reshape x4 -> x0, local copies, waits for them, and re-layouts: 8.17 us -> none  [the longest x3 6.97 us: finish(): full = full.transpose(1, 2, 0, 3).reshape(shard_rows, 4 * model_width)]
    unnamed x7 -> x11, local copies, waits for them, and re-layouts: 1.56 us -> 8.3 us
  transfers between devices with their start and end apart: 4 -> 0, of which waited for: 4 -> 0; matrix products, arithmetic and copies ran while one was open for 5% -> 0% of each run, Pallas kernels for 0% -> 0%
where the time goes in v3:
time: 148 us; the launch traced here: 147 us
  Pallas kernels  135 us (91%)
  local copies, waits for them, and re-layouts  11.7 us (8%)
    pallas_call x1, Pallas kernels, reduce_all(): pl.pallas_call(functools.partial(reduce_kernel, seq_size, dp_size), out_s...  54 us
    pallas_call x1, Pallas kernels, gather(): pl.pallas_call(functools.partial(gather_kernel, seq_size, dp_size), out_s...  53.6 us
    pallas_call x1, Pallas kernels, core(): pl.pallas_call(functools.partial(core_kernel, width // H), grid=(records,...  27.1 us
    unnamed x11, local copies, waits for them, and re-layouts  8.3 us

profile of v3, /device:TPU:0, one launch (start us, length us, event | category | flops | bytes accessed | tf_op | source)
XLA Modules:
  0.0 147.0 jit_solution(11738765153198112468)
XLA Ops:
  0.6 0.0 copy-start
  0.7 0.9 copy-done
  1.6 0.6 constant_dynamic-slice_fusion.wo
  2.2 1.5 %copy.13 = bf16[128,3072]{0,1:T(8,128)(2,1)S(1)} copy(bf16[128,3072]{1,0:T(8,128)(2,1)} %param.7) | data formatting | bytes 1572864 | tf_op args[2]
  3.8 0.8 copy.14.wq
  4.6 53.6 %shard_map.84 = (bf16[2,512,1024]{2,1,0:T(8,128)(2,1)}, bf16[2,512,1024]{2,1,0:T(8,128)(2,1)}, bf16[1024,768]{1,0:T(8,128)(2,1)}, bf16[1024,256]{1,0:T(8,128)(2,1)}, bf16[4,256,256]{2,1,0:T(8,128)(2,1)}) custom-call(bf16[2,128,1024]{2,1,0:T(8,128)(2,1)} %fr.3, bf16[2,128,1024]{2,1,0:T(8,128)(2,1)} %ct.1, bf16[128,768]{1,0:T(8,128)(2,1)} %copy.14.wq, ...), custom_call_target="tpu_custom_call" | custom-call | tf_op jit(solution)/shard_map/pallas_call | solution.py:156
  58.2 1.9 %copy.16 = bf16[4,32,8,256]{3,2,0,1:T(8,128)(2,1)} copy(bf16[4,32,8,256]{3,2,1,0:T(8,128)(2,1)} %bitcast.8) | data formatting | bytes 1048576 | tf_op jit(solution)/shard_map/reshape | solution.py:327
  60.1 27.1 %shard_map.85 = (bf16[2,512,1024]{2,1,0:T(8,128)(2,1)}, bf16[2,512,1024]{2,1,0:T(8,128)(2,1)}, bf16[1024,768]{1,0:T(8,128)(2,1)}, bf16[4,256,256]{2,1,0:T(8,128)(2,1)}) custom-call(s32[2]{0:T(128)} %lengths.1, bf16[2,512,1024]{2,1,0:T(8,128)(2,1)} %get-tuple-element.12.fr, bf16[2,512,1024]{2,1,0:T(8,128)(2,1)} %get-tuple-element.13.ct, ...), custom_call_target="tpu_custom_call" | custom-call | tf_op jit(solution)/shard_map/pallas_call | solution.py:288
  87.2 54.0 %shard_map.86 = (bf16[2,128,1024]{2,1,0:T(8,128)(2,1)}, bf16[2,128,1024]{2,1,0:T(8,128)(2,1)}, f32[128,3072]{1,0:T(8,128)}, f32[128,1024]{1,0:T(8,128)}) custom-call(bf16[2,128,1024]{2,1,0:T(8,128)(2,1)} %fr.3, bf16[2,512,1024]{2,1,0:T(8,128)(2,1)} %get-tuple-element.16.res_part, bf16[2,512,1024]{2,1,0:T(8,128)(2,1)} %get-tuple-element.17.norm_part, ...), custom_call_target="tpu_custom_call" | custom-call | tf_op jit(solution)/shard_map/pallas_call | solution.py:488
  141.2 0.0 copy-start.1
  141.2 2.0 %copy.21 = bf16[2,128,1024]{2,1,0:T(8,128)(2,1)} copy(bf16[2,128,1024]{2,1,0:T(8,128)(2,1)} %get-tuple-element.24) | data formatting | bytes 1048576
  143.2 0.0 copy-start.2
  143.2 1.9 %copy.22 = bf16[2,128,1024]{2,1,0:T(8,128)(2,1)} copy(bf16[2,128,1024]{2,1,0:T(8,128)(2,1)} %get-tuple-element.25) | data formatting | bytes 1048576
  145.1 0.0 copy-done.1
  145.1 1.1 copy.23
  146.2 0.0 copy-done.2
  146.2 0.8 copy.24
  (1 shorter events, 0.0 us)
Async XLA Ops:
  0.6 1.0 copy-start
  141.2 3.9 %copy-start.1 = (f32[128,3072]{1,0:T(8,128)S(1)}, f32[128,3072]{1,0:T(8,128)}, u32[]{:S(2)}) copy-start(f32[128,3072]{1,0:T(8,128)} %get-tuple-element.26) | copy-start | bytes 4718596
  143.2 3.1 %copy-start.2 = (f32[128,1024]{1,0:T(8,128)S(1)}, f32[128,1024]{1,0:T(8,128)}, u32[]{:S(2)}) copy-start(f32[128,1024]{1,0:T(8,128)} %get-tuple-element.27) | copy-start | bytes 1572868

commit v4 on v3

--- a/solution.py
+++ b/solution.py
@@ -66,15 +66,16 @@
         )
 
     def weight(k, src, dst_all, owner, to, slot, own):
-        place = dst_all.at[pl.ds(owner * shard, shard)]
+        first, count = ((0, shard), (0, shard // 2), (shard // 2, shard // 2))[k]
+        place = dst_all.at[pl.ds(owner * shard + first, count)]
         return pltpu.make_async_remote_copy(
-            src_ref=src if own else place, dst_ref=place,
+            src_ref=src.at[pl.ds(first, count)] if own else place, dst_ref=place,
             send_sem=w_send.at[k, slot], recv_sem=w_recv.at[k, slot],
             device_id=(to, s), device_id_type=MESH,
         )
 
     acts = ((fr, fr_all), (ct, ct_all))
-    ws = ((wo, wo_all), (wq, wq_all))
+    ws = ((wo, wo_all), (wq, wq_all), (wq, wq_all))
     across, beside, started = {}, [], []
     for k, (src, dst) in enumerate(ws):
         for d in range(1, zeds):
@@ -118,7 +119,7 @@
         return c
 
     near_out = [forward_w(0, wo_all, d) for d in range(1, zeds)]
-    late = [forward_w(1, wq_all, d) for d in range(1, zeds)]
+    late = [forward_w(k, wq_all, d) for k in (1, 2) for d in range(1, zeds)]
     late += [forward_a(0, fr_all, d) for d in range(1, outers)]
     late += [forward_a(1, ct_all, d) for d in range(1, outers)]
     local[3].wait()
@@ -164,7 +165,7 @@
         in_specs=[anywhere] * 4,
         out_specs=(anywhere,) * 5,
         scratch_shapes=[
-            dma((2, seq_size)), dma((2, seq_size)), dma((2, dp_size)), dma((2, dp_size)),
+            dma((2, seq_size)), dma((2, seq_size)), dma((3, dp_size)), dma((3, dp_size)),
             dma((seq_size,)), dma((seq_size,)), dma((5,)),
         ],
         compiler_params=pltpu.CompilerParams(collective_id=0, has_side_effects=True),
@@ -421,11 +422,11 @@
     own.start()
     hop_n.first()
     hop_r.first()
+    hop_n.second()
     own.wait()
     for c in swaps:
         c.wait_recv()
     hop_o.first()
-    hop_n.second()
     hop_q.second()
     hop_o.second()
     hop_r.second()
@@ -445,12 +446,13 @@
     each_chunk(mine_q, lambda at: put(mine_q, at, hop_q.total(at)))
     hop_o.wait()
     each_chunk(mine_o, lambda at: put(mine_o, at, hop_o.total(at)))
-    arrivals = {}
-    for d in range(1, seq_size):
-        to = lax.rem(s + d, seq_size)
-        arrivals[d] = (
-            start(mine_q, got_q.at[s], on_seq(to)), start(mine_o, got_o.at[s], on_seq(to))
-        )
+    outer, core_id, outers = s // 2, lax.rem(s, 2), seq_size // 2
+    beside = on_seq(outer * 2 + 1 - core_id)
+    arrivals, near = {}, []
+    for d in range(1, outers):
+        to = on_seq(lax.rem(outer + d, outers) * 2 + core_id)
+        arrivals[d] = (start(mine_q, got_q.at[s], to), start(mine_o, got_o.at[s], to))
+    near += [start(mine_q, got_q.at[s], beside), start(mine_o, got_o.at[s], beside)]
 
     hop_r.wait()
     each_chunk(result, lambda at: put(result, at, hop_r.total(at)))
@@ -462,9 +464,13 @@
     for c in local:
         c.start()
         c.wait()
-    for pair in arrivals.values():
-        for c in pair:
+    for d, pair in arrivals.items():
+        owner = lax.rem(outer + outers - d, outers) * 2 + core_id
+        for c, got in zip(pair, (got_q, got_o)):
             c.wait_recv()
+            near.append(start(got.at[owner], got.at[owner], beside))
+    for c in near:
+        c.wait_recv()
     for p in range(seq_size):
         for k in range(3):
             qkv_out[:, k * width + p * wide : k * width + (p + 1) * wide] = got_q[

time: 148 us -> 144 us (0.973)
  Pallas kernels: 135 us -> 132 us
    pallas_call x1, Pallas kernels: 54 us -> 50.8 us  [reduce_all(): pl.pallas_call(functools.partial(reduce_kernel, seq_size, dp_size), out_s...]
where the time goes in v4:
time: 144 us
  Pallas kernels  132 us (92%)
  local copies, waits for them, and re-layouts  11.7 us (8%)
    pallas_call x1, Pallas kernels, gather(): pl.pallas_call(functools.partial(gather_kernel, seq_size, dp_size), out_s...  53.7 us
    pallas_call x1, Pallas kernels, reduce_all(): pl.pallas_call(functools.partial(reduce_kernel, seq_size, dp_size), out_s...  50.8 us
    pallas_call x1, Pallas kernels, core(): pl.pallas_call(functools.partial(core_kernel, width // H), grid=(records,...  27.1 us
    unnamed x11, local copies, waits for them, and re-layouts  8.3 us

profile of v4, /device:TPU:0, one launch (start us, length us, event | category | flops | bytes accessed | tf_op | source)
XLA Modules:
  0.0 144.1 jit_solution(7695220177558714750)
XLA Ops:
  0.6 0.0 copy-start
  0.7 0.9 copy-done
  1.6 0.6 constant_dynamic-slice_fusion.wo
  2.2 1.5 %copy.13 = bf16[128,3072]{0,1:T(8,128)(2,1)S(1)} copy(bf16[128,3072]{1,0:T(8,128)(2,1)} %param.7) | data formatting | bytes 1572864 | tf_op args[2]
  3.8 0.8 copy.14.wq
  4.6 53.7 %shard_map.84 = (bf16[2,512,1024]{2,1,0:T(8,128)(2,1)}, bf16[2,512,1024]{2,1,0:T(8,128)(2,1)}, bf16[1024,768]{1,0:T(8,128)(2,1)}, bf16[1024,256]{1,0:T(8,128)(2,1)}, bf16[4,256,256]{2,1,0:T(8,128)(2,1)}) custom-call(bf16[2,128,1024]{2,1,0:T(8,128)(2,1)} %fr.3, bf16[2,128,1024]{2,1,0:T(8,128)(2,1)} %ct.1, bf16[128,768]{1,0:T(8,128)(2,1)} %copy.14.wq, ...), custom_call_target="tpu_custom_call" | custom-call | tf_op jit(solution)/shard_map/pallas_call | solution.py:157
  58.3 1.9 %copy.16 = bf16[4,32,8,256]{3,2,0,1:T(8,128)(2,1)} copy(bf16[4,32,8,256]{3,2,1,0:T(8,128)(2,1)} %bitcast.8) | data formatting | bytes 1048576 | tf_op jit(solution)/shard_map/reshape | solution.py:328
  60.2 27.1 %shard_map.85 = (bf16[2,512,1024]{2,1,0:T(8,128)(2,1)}, bf16[2,512,1024]{2,1,0:T(8,128)(2,1)}, bf16[1024,768]{1,0:T(8,128)(2,1)}, bf16[4,256,256]{2,1,0:T(8,128)(2,1)}) custom-call(s32[2]{0:T(128)} %lengths.1, bf16[2,512,1024]{2,1,0:T(8,128)(2,1)} %get-tuple-element.12.fr, bf16[2,512,1024]{2,1,0:T(8,128)(2,1)} %get-tuple-element.13.ct, ...), custom_call_target="tpu_custom_call" | custom-call | tf_op jit(solution)/shard_map/pallas_call | solution.py:289
  87.4 50.8 %shard_map.86 = (bf16[2,128,1024]{2,1,0:T(8,128)(2,1)}, bf16[2,128,1024]{2,1,0:T(8,128)(2,1)}, f32[128,3072]{1,0:T(8,128)}, f32[128,1024]{1,0:T(8,128)}) custom-call(bf16[2,128,1024]{2,1,0:T(8,128)(2,1)} %fr.3, bf16[2,512,1024]{2,1,0:T(8,128)(2,1)} %get-tuple-element.16.res_part, bf16[2,512,1024]{2,1,0:T(8,128)(2,1)} %get-tuple-element.17.norm_part, ...), custom_call_target="tpu_custom_call" | custom-call | tf_op jit(solution)/shard_map/pallas_call | solution.py:494
  138.2 0.0 copy-start.1
  138.2 2.0 %copy.21 = bf16[2,128,1024]{2,1,0:T(8,128)(2,1)} copy(bf16[2,128,1024]{2,1,0:T(8,128)(2,1)} %get-tuple-element.24) | data formatting | bytes 1048576
  140.2 0.0 copy-start.2
  140.2 1.9 %copy.22 = bf16[2,128,1024]{2,1,0:T(8,128)(2,1)} copy(bf16[2,128,1024]{2,1,0:T(8,128)(2,1)} %get-tuple-element.25) | data formatting | bytes 1048576
  142.1 0.0 copy-done.1
  142.1 1.1 copy.23
  143.3 0.0 copy-done.2
  143.3 0.8 copy.24
  (1 shorter events, 0.0 us)
Async XLA Ops:
  0.6 1.0 copy-start
  138.2 3.9 %copy-start.1 = (f32[128,3072]{1,0:T(8,128)S(1)}, f32[128,3072]{1,0:T(8,128)}, u32[]{:S(2)}) copy-start(f32[128,3072]{1,0:T(8,128)} %get-tuple-element.26) | copy-start | bytes 4718596
  140.2 3.1 %copy-start.2 = (f32[128,1024]{1,0:T(8,128)S(1)}, f32[128,1024]{1,0:T(8,128)}, u32[]{:S(2)}) copy-start(f32[128,1024]{1,0:T(8,128)} %get-tuple-element.27) | copy-start | bytes 1572868
